TPU v7x, 32 devices: a whole 2x2x4 slice. The times are simulated.
32 devices in a mesh: dp: 16 (over z, y, core), branch: 2 (over x).
Axes of the slice: x: 2, y: 2, z: 4, core: 2. Of those that a mesh axis runs over, the one named last changes fastest.
Arguments:
- stream: bfloat16 [16384, 1024], P(('dp', 'branch')), may hold values from -6 to 6
- cotangent: bfloat16 [16384, 1024], P(('dp', 'branch')), may hold values from -6 to 6
- lengths: int32 [16], P('dp'), may hold values from 128 to 1024, as said below
- steps_taken: int32 [1], replicated, may hold values from 2 to 20
- learning_rates: float32 [6], replicated
- mixing: float32 [1024, 3072], P(('dp', 'branch')), may hold values from -0.1875 to 0.1875
- merging: float32 [1024, 1024], P(('dp', 'branch')), may hold values from -3 to 3
- expand: float32 [1024, 4096], P(('dp', 'branch')), may hold values from -0.1875 to 0.1875
- shrink: float32 [4096, 1024], P(('dp', 'branch')), may hold values from -0.09375 to 0.09375
- vectors: float32 [2, 1024], P(None, ('dp', 'branch')), may hold values from -1 to 2
- offsets: float32 [5120], P(('dp', 'branch')), may hold values from -1.75 to 1.75
- mixing_momentum: float32 [1024, 3072], P(('dp', 'branch'))
- merging_momentum: float32 [1024, 1024], P(('dp', 'branch'))
- expand_momentum: float32 [1024, 4096], P(('dp', 'branch'))
- shrink_momentum: float32 [4096, 1024], P(('dp', 'branch'))
- vectors_momentum: float32 [2, 1024], P(None, ('dp', 'branch'))
- offsets_momentum: float32 [5120], P(('dp', 'branch'))
- mixing_variance: float32 [1024, 3072], P(('dp', 'branch'))
- merging_variance: float32 [1024, 1024], P(('dp', 'branch'))
- expand_variance: float32 [1024, 4096], P(('dp', 'branch'))
- shrink_variance: float32 [4096, 1024], P(('dp', 'branch'))
- vectors_variance: float32 [2, 1024], P(None, ('dp', 'branch'))
- offsets_variance: float32 [5120], P(('dp', 'branch'))
Outputs:
- residual: bfloat16 [16384, 1024], P(('dp', 'branch'))
- stream_grad: float32 [16384, 1024], P(('dp', 'branch'))
- mixing_next: float32 [1024, 3072], P(('dp', 'branch'))
- mixing_half: bfloat16 [1024, 3072], P(('dp', 'branch'))
- mixing_drift: float32 [1024, 3072], P(('dp', 'branch'))
- mixing_power: float32 [1024, 3072], P(('dp', 'branch'))
- merging_next: float32 [1024, 1024], P(('dp', 'branch'))
- merging_half: bfloat16 [1024, 1024], P(('dp', 'branch'))
- merging_drift: float32 [1024, 1024], P(('dp', 'branch'))
- merging_power: float32 [1024, 1024], P(('dp', 'branch'))
- expand_next: float32 [1024, 4096], P(('dp', 'branch'))
- expand_half: bfloat16 [1024, 4096], P(('dp', 'branch'))
- expand_drift: float32 [1024, 4096], P(('dp', 'branch'))
- expand_power: float32 [1024, 4096], P(('dp', 'branch'))
- shrink_next: float32 [4096, 1024], P(('dp', 'branch'))
- shrink_half: bfloat16 [4096, 1024], P(('dp', 'branch'))
- shrink_drift: float32 [4096, 1024], P(('dp', 'branch'))
- shrink_power: float32 [4096, 1024], P(('dp', 'branch'))
- vectors_next: float32 [2, 1024], P(None, ('dp', 'branch'))
- vectors_half: bfloat16 [2, 1024], P(None, ('dp', 'branch'))
- vectors_drift: float32 [2, 1024], P(None, ('dp', 'branch'))
- vectors_power: float32 [2, 1024], P(None, ('dp', 'branch'))
- offsets_next: float32 [5120], P(('dp', 'branch'))
- offsets_half: bfloat16 [5120], P(('dp', 'branch'))
- offsets_drift: float32 [5120], P(('dp', 'branch'))
- offsets_power: float32 [5120], P(('dp', 'branch'))
Inputs may be any that keep to these rules, and one draw needn't show every extreme that they name: `lengths`: at least one protein of all has exactly 1024 residues.
All inputs are finite; a program needn't handle non-finite values.
Results may differ from a plain program's by a relative error of at most 0.01.
The roundings to bfloat16 on the way count: a program that leaves them out, or rounds other values in their place, can miss the bound.
Values may be sent and summed in bfloat16 or wider, within the bound.
A program may use at most 256 MiB of HBM per device.

v0:
```python
import jax
import jax.numpy as jnp
from jax import lax
from jax.sharding import PartitionSpec as P

HEADS = 16
HEAD = 64
ROT = 32


beta_one = 0.9
beta_two = 0.95
adam_eps = 1e-08
decay_rate = 0.1
norm_eps = 1e-05
rope_base = 10000.0
masked_score = -1e30


def rope_tables(length, head_dim, rot_dim):
    places = jnp.arange(length).astype(jnp.float32)[:, None]
    column = jnp.arange(head_dim)
    paired = (column // 2).astype(jnp.float32)
    frequency = jnp.exp(paired * (-2.0 / rot_dim) * jnp.log(rope_base))
    angles = places * frequency[None, :]
    inside = (column < rot_dim)[None, :]
    cosine = jnp.where(inside, jnp.cos(angles), 1.0)
    signed = jnp.where(column % 2 == 0, -1.0, 1.0)[None, :]
    sine = jnp.where(inside, jnp.sin(angles) * signed, 0.0)
    return (cosine[:, None, :], sine[:, None, :])


def swap_pairs(tensor):
    shaped = tensor.reshape(tensor.shape[:-1] + (tensor.shape[-1] // 2, 2))
    return jnp.flip(shaped, axis=-1).reshape(tensor.shape)


def rotate(tensor, cosine, sine):
    return tensor * cosine + swap_pairs(tensor) * sine


def rotate_back(tensor, cosine, sine):
    return tensor * cosine + swap_pairs(tensor * sine)


def product(left, right):
    return jnp.dot(left, right, preferred_element_type=jnp.float32)


def product_left(left, right):
    return lax.dot_general(
        left, right, (((0,), (0,)), ((), ())), preferred_element_type=jnp.float32
    )


def product_right(left, right):
    return lax.dot_general(
        left, right, (((1,), (1,)), ((), ())), preferred_element_type=jnp.float32
    )


def gelu_tanh(tensor):
    return jax.nn.gelu(tensor, approximate=True)


def adam_update(master, gradient, momentum, variance, rate, count, decay):
    drift = beta_one * momentum + (1.0 - beta_one) * gradient
    power = beta_two * variance + (1.0 - beta_two) * gradient * gradient
    first_fix = 1.0 - jnp.power(beta_one, count)
    second_fix = 1.0 - jnp.power(beta_two, count)
    moved = drift / first_fix / (jnp.sqrt(power / second_fix) + adam_eps)
    updated = master - rate * (moved + decay * master)
    return (updated, updated.astype(jnp.bfloat16), drift, power)


def attend(normed_seq, grad_seq, length, mixing_w, merging_w, cosine, sine):
    padded, model_width = normed_seq.shape
    block_size = min(512, padded)
    block_count = padded // block_size
    score_scale = HEAD ** (-0.5)
    projected = product(normed_seq, mixing_w)
    query_rows = rotate(
        projected[:, :model_width].reshape(padded, HEADS, HEAD), cosine, sine
    ).astype(jnp.bfloat16)
    key_rows = rotate(
        projected[:, model_width : 2 * model_width].reshape(padded, HEADS, HEAD), cosine, sine
    ).astype(jnp.bfloat16)
    value_rows = projected[:, 2 * model_width :].reshape(padded, HEADS, HEAD).astype(jnp.bfloat16)
    positions = jnp.arange(padded)
    live_rows = positions < length
    causal = positions[:block_size, None] >= positions[None, :block_size]

    def scores_of(row_block, col_block):
        queries = query_rows[row_block * block_size : (row_block + 1) * block_size]
        lookups = key_rows[col_block * block_size : (col_block + 1) * block_size]
        scores = (
            jnp.einsum("qhd,khd->hqk", queries, lookups, preferred_element_type=jnp.float32)
            * score_scale
        )
        if row_block == col_block:
            scores = jnp.where(causal[None], scores, masked_score)
        return scores

    mixed_parts = []
    leftover_parts = []
    total_parts = []
    for row_block in range(block_count):

        def live_forward(unused):
            running_max = jnp.full((HEADS, block_size), masked_score, jnp.float32)
            running_sum = jnp.zeros((HEADS, block_size), jnp.float32)
            for col_block in range(row_block + 1):
                scores = scores_of(row_block, col_block)
                new_max = jnp.maximum(running_max, jnp.max(scores, axis=2))
                running_sum = running_sum * jnp.exp(running_max - new_max) + jnp.sum(
                    jnp.exp(scores - new_max[:, :, None]), axis=2
                )
                running_max = new_max
            log_total = running_max + jnp.log(running_sum)
            mixed = jnp.zeros((block_size, HEADS, HEAD), jnp.float32)
            remainder = jnp.zeros((block_size, HEADS, HEAD), jnp.float32)
            for col_block in range(row_block + 1):
                weights = jnp.exp(scores_of(row_block, col_block) - log_total[:, :, None])
                rounded = weights.astype(jnp.bfloat16)
                leftover = (weights - rounded.astype(jnp.float32)).astype(jnp.bfloat16)
                picked = value_rows[col_block * block_size : (col_block + 1) * block_size]
                mixed = mixed + jnp.einsum(
                    "hqk,khd->qhd", rounded, picked, preferred_element_type=jnp.float32
                )
                remainder = remainder + jnp.einsum(
                    "hqk,khd->qhd", leftover, picked, preferred_element_type=jnp.float32
                )
            return (mixed, remainder, log_total)

        def dead_forward(unused):
            return (
                jnp.zeros((block_size, HEADS, HEAD), jnp.float32),
                jnp.zeros((block_size, HEADS, HEAD), jnp.float32),
                jnp.zeros((HEADS, block_size), jnp.float32),
            )

        mixed, remainder, log_total = lax.cond(
            row_block * block_size < length, live_forward, dead_forward, 0
        )
        mixed_parts.append(mixed)
        leftover_parts.append(remainder)
        total_parts.append(log_total)
    attn_high = jnp.concatenate(mixed_parts, axis=0)
    attn_rest = jnp.concatenate(leftover_parts, axis=0)
    log_totals = jnp.concatenate(total_parts, axis=1)
    mask_rows = live_rows[:, None, None]
    attention = (
        jnp.where(mask_rows, attn_high, 0.0).astype(jnp.bfloat16).reshape(padded, model_width)
    )
    branch_out = product(attention, merging_w).astype(jnp.bfloat16).astype(jnp.float32)
    grad_merging = product_left(attention, grad_seq)
    grad_attention = (
        product_right(grad_seq, merging_w).astype(jnp.bfloat16).reshape(padded, HEADS, HEAD)
    )
    exact_mix = jnp.where(mask_rows, attn_high + attn_rest, 0.0)
    deltas = jnp.sum(grad_attention.astype(jnp.float32) * exact_mix, axis=2).T
    grad_query = jnp.zeros((padded, HEADS, HEAD), jnp.float32)
    grad_key = jnp.zeros((padded, HEADS, HEAD), jnp.float32)
    grad_value = jnp.zeros((padded, HEADS, HEAD), jnp.float32)
    for row_block in range(block_count):

        def live_backward(kept_grads):
            query_acc, key_acc, value_acc = kept_grads
            lower = row_block * block_size
            upper = lower + block_size
            totals = log_totals[:, lower:upper]
            shifts = deltas[:, lower:upper]
            incoming = grad_attention[lower:upper]
            queries = query_rows[lower:upper]
            block_query = jnp.zeros((block_size, HEADS, HEAD), jnp.float32)
            for col_block in range(row_block + 1):
                start = col_block * block_size
                stop = start + block_size
                weights = jnp.exp(scores_of(row_block, col_block) - totals[:, :, None])
                value_acc = value_acc.at[start:stop].add(
                    jnp.einsum(
                        "hqk,qhd->khd",
                        weights.astype(jnp.bfloat16),
                        incoming,
                        preferred_element_type=jnp.float32,
                    )
                )
                grad_weights = jnp.einsum(
                    "qhd,khd->hqk",
                    incoming,
                    value_rows[start:stop],
                    preferred_element_type=jnp.float32,
                )
                grad_scores = (weights * (grad_weights - shifts[:, :, None])).astype(jnp.bfloat16)
                block_query = (
                    block_query
                    + jnp.einsum(
                        "hqk,khd->qhd",
                        grad_scores,
                        key_rows[start:stop],
                        preferred_element_type=jnp.float32,
                    )
                    * score_scale
                )
                key_acc = key_acc.at[start:stop].add(
                    jnp.einsum(
                        "hqk,qhd->khd", grad_scores, queries, preferred_element_type=jnp.float32
                    )
                    * score_scale
                )
            query_acc = query_acc.at[lower:upper].set(block_query)
            return (query_acc, key_acc, value_acc)

        def dead_backward(kept_grads):
            return kept_grads

        grad_query, grad_key, grad_value = lax.cond(
            row_block * block_size < length,
            live_backward,
            dead_backward,
            (grad_query, grad_key, grad_value),
        )
    grad_proj = jnp.concatenate(
        [
            rotate_back(grad_query, cosine, sine).reshape(padded, model_width),
            rotate_back(grad_key, cosine, sine).reshape(padded, model_width),
            grad_value.reshape(padded, model_width),
        ],
        axis=1,
    ).astype(jnp.bfloat16)
    grad_mixing = product_left(normed_seq, grad_proj)
    grad_normed = product_right(grad_proj, mixing_w)
    return (branch_out, grad_normed, grad_mixing, grad_merging)


def local(
    stream,
    cotangent,
    lengths,
    steps_taken,
    learning_rates,
    mixing,
    merging,
    expand,
    shrink,
    vectors,
    offsets,
    mixing_momentum,
    merging_momentum,
    expand_momentum,
    shrink_momentum,
    vectors_momentum,
    offsets_momentum,
    mixing_variance,
    merging_variance,
    expand_variance,
    shrink_variance,
    vectors_variance,
    offsets_variance,
):
    gathered = (
        lax.all_gather(mixing.astype(jnp.bfloat16), ("dp", "branch"), axis=0, tiled=True),
        lax.all_gather(merging.astype(jnp.bfloat16), ("dp", "branch"), axis=0, tiled=True),
        lax.all_gather(expand.astype(jnp.bfloat16), ("dp", "branch"), axis=0, tiled=True),
        lax.all_gather(shrink.astype(jnp.bfloat16), ("dp", "branch"), axis=0, tiled=True),
        lax.all_gather(vectors.astype(jnp.bfloat16), ("dp", "branch"), axis=1, tiled=True),
        lax.all_gather(offsets.astype(jnp.bfloat16), ("dp", "branch"), axis=0, tiled=True),
    )
    mixing_w, merging_w, expand_w, shrink_w, vector_w, offset_w = gathered
    hidden_width = expand_w.shape[1]
    norm_gain = vector_w[0].astype(jnp.float32)
    norm_shift = vector_w[1].astype(jnp.float32)
    offset_bias = offset_w[:hidden_width].astype(jnp.float32)
    tail_bias = offset_w[hidden_width:].astype(jnp.float32)
    inputs = stream.astype(jnp.float32)
    centred = inputs - jnp.mean(inputs, axis=1, keepdims=True)
    inverse = lax.rsqrt(jnp.mean(centred * centred, axis=1, keepdims=True) + norm_eps)
    standard = centred * inverse
    normed_own = (standard * norm_gain + norm_shift).astype(jnp.bfloat16)
    normed = lax.all_gather(normed_own, "branch", axis=0, tiled=True)
    grads_all = lax.all_gather(cotangent, "branch", axis=0, tiled=True)
    group_rows, model_width = normed.shape
    seq_count = lengths.shape[0]
    padded = group_rows // seq_count
    positions = jnp.arange(padded)
    live_rows = (positions[None, :] < lengths[:, None]).reshape(group_rows)
    grads_masked = jnp.where(live_rows[:, None], grads_all, jnp.zeros_like(grads_all))
    branch_index = lax.axis_index("branch")

    def attention_side(unused):
        cosine, sine = rope_tables(padded, HEAD, ROT)

        def per_sequence(carried, sequence_in):
            normed_seq, grad_seq, length = sequence_in
            branch_out, grad_normed, grad_mix, grad_merge = attend(
                normed_seq, grad_seq, length, mixing_w, merging_w, cosine, sine
            )
            return ((carried[0] + grad_mix, carried[1] + grad_merge), (branch_out, grad_normed))

        initial = (jnp.zeros(mixing_w.shape, jnp.float32), jnp.zeros(merging_w.shape, jnp.float32))
        sums, rows_out = lax.scan(
            per_sequence,
            initial,
            (
                normed.reshape(seq_count, padded, model_width),
                grads_masked.reshape(seq_count, padded, model_width),
                lengths,
            ),
        )
        return (
            rows_out[0].reshape(group_rows, model_width),
            rows_out[1].reshape(group_rows, model_width),
            sums[0],
            sums[1],
            jnp.zeros(expand_w.shape, jnp.float32),
            jnp.zeros(shrink_w.shape, jnp.float32),
            jnp.zeros(offset_w.shape, jnp.float32),
        )

    def feed_side(unused):
        block_rows = min(1024, group_rows)
        block_total = group_rows // block_rows

        def per_block(carried, block_in):
            normed_part, grad_part = block_in
            before_gelu = product(normed_part, expand_w) + offset_bias
            activated, gelu_back = jax.vjp(gelu_tanh, before_gelu)
            hidden = activated.astype(jnp.bfloat16)
            branch_out = (
                (product(hidden, shrink_w) + tail_bias).astype(jnp.bfloat16).astype(jnp.float32)
            )
            grad_hidden = product_right(grad_part, shrink_w)
            grad_pre = gelu_back(grad_hidden)[0].astype(jnp.bfloat16)
            grad_normed = product_right(grad_pre, expand_w)
            updated = (
                carried[0] + product_left(normed_part, grad_pre),
                carried[1] + product_left(hidden, grad_part),
                carried[2] + jnp.sum(grad_pre.astype(jnp.float32), axis=0),
                carried[3] + jnp.sum(grad_part.astype(jnp.float32), axis=0),
            )
            return (updated, (branch_out, grad_normed))

        initial = (
            jnp.zeros(expand_w.shape, jnp.float32),
            jnp.zeros(shrink_w.shape, jnp.float32),
            jnp.zeros((hidden_width,), jnp.float32),
            jnp.zeros((model_width,), jnp.float32),
        )
        sums, rows_out = lax.scan(
            per_block,
            initial,
            (
                normed.reshape(block_total, block_rows, model_width),
                grads_masked.reshape(block_total, block_rows, model_width),
            ),
        )
        bias_grads = jnp.concatenate([sums[2], sums[3]], axis=0)
        return (
            rows_out[0].reshape(group_rows, model_width),
            rows_out[1].reshape(group_rows, model_width),
            jnp.zeros(mixing_w.shape, jnp.float32),
            jnp.zeros(merging_w.shape, jnp.float32),
            sums[0],
            sums[1],
            bias_grads,
        )

    branch_rows, dnorm_rows, grad_mixing, grad_merging, grad_expand, grad_shrink, grad_offsets = (
        lax.cond(branch_index == 0, attention_side, feed_side, 0)
    )
    own_rows = stream.shape[0]
    summed = lax.psum_scatter(
        branch_rows.astype(jnp.bfloat16), "branch", scatter_dimension=0, tiled=True
    ).astype(jnp.float32)
    residual = (inputs + summed).astype(jnp.bfloat16)
    dnorm_own = lax.psum_scatter(
        dnorm_rows.astype(jnp.bfloat16), "branch", scatter_dimension=0, tiled=True
    ).astype(jnp.float32)
    own_grads = lax.dynamic_slice_in_dim(grads_masked, branch_index * own_rows, own_rows, 0).astype(
        jnp.float32
    )
    grad_gain = jnp.sum(dnorm_own * standard, axis=0)
    grad_shift = jnp.sum(dnorm_own, axis=0)
    grad_unit = dnorm_own * norm_gain
    stream_grad = own_grads + inverse * (
        grad_unit
        - jnp.mean(grad_unit, axis=1, keepdims=True)
        - standard * jnp.mean(grad_unit * standard, axis=1, keepdims=True)
    )
    grad_vectors = jnp.stack([grad_gain, grad_shift])
    reduced = (
        lax.psum_scatter(grad_mixing, ("dp", "branch"), scatter_dimension=0, tiled=True),
        lax.psum_scatter(grad_merging, ("dp", "branch"), scatter_dimension=0, tiled=True),
        lax.psum_scatter(grad_expand, ("dp", "branch"), scatter_dimension=0, tiled=True),
        lax.psum_scatter(grad_shrink, ("dp", "branch"), scatter_dimension=0, tiled=True),
        lax.psum_scatter(grad_vectors, ("dp", "branch"), scatter_dimension=1, tiled=True),
        lax.psum_scatter(grad_offsets, ("dp", "branch"), scatter_dimension=0, tiled=True),
    )
    count = steps_taken[0].astype(jnp.float32)
    mixing_next, mixing_half, mixing_drift, mixing_power = adam_update(
        mixing, reduced[0], mixing_momentum, mixing_variance, learning_rates[0], count, decay_rate
    )
    merging_next, merging_half, merging_drift, merging_power = adam_update(
        merging,
        reduced[1],
        merging_momentum,
        merging_variance,
        learning_rates[1],
        count,
        decay_rate,
    )
    expand_next, expand_half, expand_drift, expand_power = adam_update(
        expand, reduced[2], expand_momentum, expand_variance, learning_rates[2], count, decay_rate
    )
    shrink_next, shrink_half, shrink_drift, shrink_power = adam_update(
        shrink, reduced[3], shrink_momentum, shrink_variance, learning_rates[3], count, decay_rate
    )
    vectors_next, vectors_half, vectors_drift, vectors_power = adam_update(
        vectors, reduced[4], vectors_momentum, vectors_variance, learning_rates[4], count, 0.0
    )
    offsets_next, offsets_half, offsets_drift, offsets_power = adam_update(
        offsets, reduced[5], offsets_momentum, offsets_variance, learning_rates[5], count, 0.0
    )
    return (
        residual,
        stream_grad,
        mixing_next,
        mixing_half,
        mixing_drift,
        mixing_power,
        merging_next,
        merging_half,
        merging_drift,
        merging_power,
        expand_next,
        expand_half,
        expand_drift,
        expand_power,
        shrink_next,
        shrink_half,
        shrink_drift,
        shrink_power,
        vectors_next,
        vectors_half,
        vectors_drift,
        vectors_power,
        offsets_next,
        offsets_half,
        offsets_drift,
        offsets_power,
    )


def solution(mesh):
    return jax.shard_map(
        local,
        mesh=mesh,
        in_specs=(
            P(("dp", "branch"), None),
            P(("dp", "branch"), None),
            P("dp"),
            P(),
            P(),
            P(("dp", "branch"), None),
            P(("dp", "branch"), None),
            P(("dp", "branch"), None),
            P(("dp", "branch"), None),
            P(None, ("dp", "branch")),
            P(("dp", "branch")),
            P(("dp", "branch"), None),
            P(("dp", "branch"), None),
            P(("dp", "branch"), None),
            P(("dp", "branch"), None),
            P(None, ("dp", "branch")),
            P(("dp", "branch")),
            P(("dp", "branch"), None),
            P(("dp", "branch"), None),
            P(("dp", "branch"), None),
            P(("dp", "branch"), None),
            P(None, ("dp", "branch")),
            P(("dp", "branch")),
        ),
        out_specs=(
            P(("dp", "branch"), None),
            P(("dp", "branch"), None),
            P(("dp", "branch"), None),
            P(("dp", "branch"), None),
            P(("dp", "branch"), None),
            P(("dp", "branch"), None),
            P(("dp", "branch"), None),
            P(("dp", "branch"), None),
            P(("dp", "branch"), None),
            P(("dp", "branch"), None),
            P(("dp", "branch"), None),
            P(("dp", "branch"), None),
            P(("dp", "branch"), None),
            P(("dp", "branch"), None),
            P(("dp", "branch"), None),
            P(("dp", "branch"), None),
            P(("dp", "branch"), None),
            P(("dp", "branch"), None),
            P(None, ("dp", "branch")),
            P(None, ("dp", "branch")),
            P(None, ("dp", "branch")),
            P(None, ("dp", "branch")),
            P(("dp", "branch")),
            P(("dp", "branch")),
            P(("dp", "branch")),
            P(("dp", "branch")),
        ),
        check_vma=False,
    )
```

profile of v0, /device:TPU:0, one launch (start us, length us, event | category | flops | bytes accessed | tf_op | source)
XLA Modules:
  0.0 2153.4 jit_solution(18214619501647290868)
XLA Ops:
  8.7 69.3 %all-gather = bf16[32,32,2]{1,2,0:T(2,128)(2,1)S(1)} all-gather(bf16[1,32,2]{1,2,0:T(2,128)(2,1)S(1)} %convert_bitcast_fusion), channel_id=1, replica_groups=mesh['dp'=16,'branch'=2] {'dp','branch'}, dimensions={0}, use_global_device_ids=true | all-gather | bytes 4224 | tf_op jit(solution)/shard_map/all_gather | solution.py:266
  81.8 2.6 fusion.147
  88.7 37.4 %all-reduce.3 = bf16[5120]{0:T(1024)(128)(2,1)S(1)} all-reduce(bf16[5120]{0:T(1024)(128)(2,1)S(1)} %dynamic-update-slice.24), channel_id=1, replica_groups=mesh['dp'=16,'branch'=2] {'dp','branch'}, use_global_device_ids=true, to_apply=%add.3 | all-reduce | flops 5120 | bytes 20480
  126.1 3.2 broadcast_select_fusion
  129.2 44.7 %all-gather.18.cloned.1.call-done = bf16[1024,1024]{1,0:T(8,128)(2,1)} async-done(((bf16[32,1024]{1,0:T(8,128)(2,1)}), bf16[1024,1024]{1,0:T(8,128)(2,1)}) %all-gather.18.cloned.1.call-update) | async-done | bytes 2097168 | tf_op jit(solution)/shard_map/all_gather | solution.py:263
  174.0 71.7 %all-gather.16.cloned.1.call-done = bf16[1024,3072]{1,0:T(8,128)(2,1)} async-done(((bf16[32,3072]{1,0:T(8,128)(2,1)}), bf16[1024,3072]{1,0:T(8,128)(2,1)}) %all-gather.16.cloned.1.call-update) | async-done | bytes 6291472 | tf_op jit(solution)/shard_map/all_gather | solution.py:262
  245.7 79.2 %all-gather.10.cloned.1.call-done = bf16[1024,4096]{1,0:T(8,128)(2,1)} async-done(((bf16[32,4096]{1,0:T(8,128)(2,1)}), bf16[1024,4096]{1,0:T(8,128)(2,1)}) %all-gather.10.cloned.1.call-update) | async-done | bytes 8388624 | tf_op jit(solution)/shard_map/all_gather | solution.py:264
  324.9 79.3 %all-gather.12.cloned.1.call-done = bf16[4096,1024]{1,0:T(8,128)(2,1)} async-done(((bf16[128,1024]{1,0:T(8,128)(2,1)}), bf16[4096,1024]{1,0:T(8,128)(2,1)}) %all-gather.12.cloned.1.call-update) | async-done | bytes 8388624 | tf_op jit(solution)/shard_map/all_gather | solution.py:265
  404.2 376.3 %conditional.5 = (bf16[1024,1024]{1,0:T(8,128)(2,1)}, bf16[1024,1024]{1,0:T(8,128)(2,1)}, f32[1024,3072]{0,1:T(8,128)}, f32[1024,1024]{1,0:T(8,128)}, f32[1024,4...) conditional(s32[]{:T(128)} %convert_element_type.235, (bf16[1024,1024]{1,0:T(8,128)(2,1)}, ...), branch_computations={%region_2.5_spmd, %region_5.21_spmd} | conditional | flops 51724156928 | bytes 1273409792 | solution.py:369
  412.7 9.4 fusion.178
  422.1 4.8 fusion.174
  429.3 5.3 copy.106
  434.7 5.8 reshape.574
  440.5 20.9 rev.13
  461.4 6.1 reshape.575
  467.5 5.4 copy.108
  472.9 5.8 reshape.577
  478.7 21.0 rev.14
  499.7 6.0 reshape.578
  506.8 9.7 add_convert_fusion.3
  516.5 3.9 slice.406
  520.4 3.9 copy.110
  525.2 40.4 %conditional = (f32[512,16,64]{0,2,1:T(8,128)}, f32[512,16,64]{0,2,1:T(8,128)}, f32[16,512]{1,0:T(8,128)}, f32[512,1024]{0,1:T(8,128)}) conditional(s32[]{:T(128)} %convert_element_type.184, () %tuple.80, (pred[512,512]{1,0:T(8,128)(4,1)S(1)}, bf16[1024,16,64]{0,2,1:T(8,128)(2,1)S(1)}, bf16[1024,16,64]{0,2,1:T(8,128)(2,1)}, ...), branch_computations={%region_6.6_spmd, %region_7.9_spmd} | conditional | flops 1686142976 | bytes 157089888 | solution.py:142
  526.0 8.7 fusion.10
  534.8 9.2 exponential_reduce_fusion
  544.6 11.6 fusion.11
  556.2 3.2 copy.143
  559.4 6.2 fusion.19
  566.3 15.2 conditional.1
  582.2 8.7 fusion.122
  590.9 42.8 %conditional.2 = (f32[1024,16,64]{0,2,1:T(8,128)}, f32[1024,16,64]{0,2,1:T(8,128)S(1)}, f32[1024,16,64]{0,2,1:T(8,128)S(1)}) conditional(s32[]{:T(128)} %convert_element_type.184, () %tuple.84, (pred[512,512]{1,0:T(8,128)(4,1)S(1)}, bf16[1024,16,64]{0,2,1:T(8,128)(2,1)S(1)}, bf16[1024,16,64]{0,2,1:T(8,128)(2,1)S(1)}, f32[16,512]{1,0:T(8,128)}, ...), branch_computations={%region_17.17_spmd, %region_18.18_spmd} | conditional | flops 2727346176 | bytes 125468760 | solution.py:217
  590.9 8.2 fusion.76
  599.1 11.9 multiply_convert_fusion.3
  611.0 4.8 multiply_bitcast_fusion
  616.3 6.0 multiply_bitcast_fusion.1
  622.4 2.6 scatter.4
  625.0 8.2 fusion.69
  633.7 10.0 conditional.3
  643.8 8.5 broadcast_multiply_fusion.1
  652.3 5.8 reshape.580
  658.2 21.0 rev.15
  679.2 6.1 reshape.581
  685.3 5.8 reshape.583
  691.1 21.0 rev.16
  712.1 6.1 reshape.584
  718.2 8.3 add_convert_fusion.2
  726.6 12.9 convolution_bitcast_fusion.1
  739.5 7.2 fusion.127
  746.7 11.3 fusion.123
  757.9 5.9 convert_convert_fusion
  763.9 7.9 broadcast.458
  771.8 7.9 broadcast.459
  781.4 169.8 %reduce-scatter.12.cloned.1.call-done = bf16[512,1024]{1,0:T(8,128)(2,1)} async-done(((bf16[1024,1024]{1,0:T(8,128)(2,1)}), bf16[512,1024]{1,0:T(8,128)(2,1)}) %reduce-scatter.12.cloned.1.call-update) | async-done | bytes 1048592 | tf_op jit(solution)/shard_map/reduce_scatter | solution.py:376
  955.2 12.7 copy.114
  970.6 39.9 %all-reduce.4 = f32[5120]{0:T(1024)S(1)} all-reduce(f32[5120]{0:T(1024)} %get-tuple-element.350), channel_id=9, replica_groups=mesh['dp'=16,'branch'=2] {'dp','branch'}, use_global_device_ids=true, to_apply=%region_32.33.clone | all-reduce | flops 5120 | bytes 40960
  1012.4 4.2 fusion.150
  1016.6 107.0 %reduce-scatter.22.cloned.1.call-done = f32[32,2]{1,0:T(8,128)} async-done(((f32[1024,2]{1,0:T(8,128)}), f32[32,2]{1,0:T(8,128)}) %reduce-scatter.22.cloned.1.call-update) | async-done | bytes 272
  1126.3 137.4 %reduce-scatter.16.cloned.1.call-done = f32[32,1024]{1,0:T(8,128)} async-done(((f32[1024,1024]{1,0:T(8,128)}), f32[32,1024]{1,0:T(8,128)}) %reduce-scatter.16.cloned.1.call-update) | async-done | bytes 131088 | tf_op jit(solution)/shard_map/reduce_scatter | solution.py:393
  1266.2 157.7 %reduce-scatter.14.cloned.1.call-done = f32[32,3072]{1,0:T(8,128)} async-done(((f32[1024,3072]{1,0:T(8,128)}), f32[32,3072]{1,0:T(8,128)}) %reduce-scatter.14.cloned.1.call-update) | async-done | bytes 393232 | tf_op jit(solution)/shard_map/reduce_scatter | solution.py:392
  1424.0 3.1 fusion.172
  1427.1 355.5 %reduce-scatter.20.cloned.1.call-done = f32[128,1024]{1,0:T(8,128)} async-done(((f32[4096,1024]{1,0:T(8,128)}), f32[128,1024]{1,0:T(8,128)}) %reduce-scatter.20.cloned.1.call-update) | async-done | bytes 524304 | tf_op jit(solution)/shard_map/reduce_scatter | solution.py:395
  1782.6 3.2 fusion.166
  1785.7 357.8 %reduce-scatter.18.cloned.1.call-done = f32[32,4096]{1,0:T(8,128)} async-done(((f32[1024,4096]{1,0:T(8,128)}), f32[32,4096]{1,0:T(8,128)}) %reduce-scatter.18.cloned.1.call-update) | async-done | bytes 524304 | tf_op jit(solution)/shard_map/reduce_scatter | solution.py:394
  2143.5 3.1 fusion.168
  (150 shorter events, 36.2 us)
Async XLA Ops:
  7.2 77.3 %copy-start.39 = (f32[32,1024]{1,0:T(8,128)S(1)}, f32[32,1024]{1,0:T(8,128)}, u32[]{:S(2)}) copy-start(f32[32,1024]{1,0:T(8,128)} %param.55) | copy-start | bytes 393220
  7.2 78.1 %copy-start.31 = (f32[32,3072]{1,0:T(8,128)S(1)}, f32[32,3072]{1,0:T(8,128)}, u32[]{:S(2)}) copy-start(f32[32,3072]{1,0:T(8,128)} %param.54) | copy-start | bytes 1179652
  7.2 78.8 %copy-start.28 = (f32[32,4096]{1,0:T(8,128)S(1)}, f32[32,4096]{1,0:T(8,128)}, u32[]{:S(2)}) copy-start(f32[32,4096]{1,0:T(8,128)} %param.56) | copy-start | bytes 1572868
  7.2 79.6 %copy-start.26 = (f32[128,1024]{1,0:T(8,128)S(1)}, f32[128,1024]{1,0:T(8,128)}, u32[]{:S(2)}) copy-start(f32[128,1024]{1,0:T(8,128)} %param.57) | copy-start | bytes 1572868
  7.2 118.8 %all-gather.14.cloned.1.call-start = ((), (), s32[]{:S(2)}) async-start(), calls=%async_computation.10 | async-start | bytes 3145728 | tf_op jit(solution)/shard_map/all_gather | solution.py:281
  8.0 121.3 %all-gather.8.cloned.1.call-start = ((), (), s32[]{:S(2)}) async-start(), calls=%async_computation.7 | async-start | bytes 3145728 | tf_op jit(solution)/shard_map/all_gather | solution.py:280
  78.1 10.3 copy-start.47
  79.5 1.7 copy-start.42
  81.2 48.0 %copy-start.44 = (f32[512]{0:T(512)}, f32[512]{0:T(512)S(1)}, u32[]{:S(2)}) copy-start(f32[512]{0:T(512)S(1)} %add_rsqrt_fusion) | copy-start | bytes 6148
  81.2 0.6 copy-start.40
  84.5 89.5 %all-gather.18.cloned.1.call-start = ((), (), s32[]{:S(2)}) async-start(), calls=%async_computation.12 | async-start | bytes 2162688 | tf_op jit(solution)/shard_map/all_gather | solution.py:263
  85.2 160.5 %all-gather.16.cloned.1.call-start = ((), (), s32[]{:S(2)}) async-start(), calls=%async_computation.11 | async-start | bytes 6488064 | tf_op jit(solution)/shard_map/all_gather | solution.py:262
  86.0 238.9 %all-gather.10.cloned.1.call-start = ((), (), s32[]{:S(2)}) async-start(), calls=%async_computation.8 | async-start | bytes 8650752 | tf_op jit(solution)/shard_map/all_gather | solution.py:264
  86.8 317.4 %all-gather.12.cloned.1.call-start = ((), (), s32[]{:S(2)}) async-start(), calls=%async_computation.9 | async-start | bytes 8650752 | tf_op jit(solution)/shard_map/all_gather | solution.py:265
  87.7 863.6 %reduce-scatter.12.cloned.1.call-start = ((), (), s32[]{:S(2)}) async-start(), calls=%async_computation.14 | async-start | bytes 3145728 | tf_op jit(solution)/shard_map/reduce_scatter | solution.py:376
  422.1 7.2 copy-start.18
  506.8 9.7 copy-start.22
  506.8 9.7 copy-start.24
  544.6 14.9 copy-start.7
  556.2 3.3 copy-start.15
  582.2 8.7 copy-start.8
  590.9 8.2 copy-start.17
  590.9 8.2 copy-start.19
  633.7 10.1 copy-start.23
  643.8 8.6 copy-start.4
  712.1 6.1 copy-start.25
  718.2 8.3 copy-start.52
  746.7 11.3 copy-start.30
  780.6 170.7 %copy-start.14 = (bf16[512,1024]{1,0:T(8,128)(2,1)S(1)}, bf16[512,1024]{1,0:T(8,128)(2,1)}, u32[]{:S(2)}) copy-start(bf16[512,1024]{1,0:T(8,128)(2,1)} %param.49) | copy-start | bytes 3145732
  780.6 170.7 %copy-start.41 = (f32[1,1024]{1,0:T(1,128)S(1)}, f32[1,1024]{1,0:T(1,128)}, u32[]{:S(2)}) copy-start(f32[1,1024]{1,0:T(1,128)} %copy-done.40) | copy-start | bytes 12292
  780.6 170.7 %copy-start.43 = (f32[512]{0:T(512)S(1)}, f32[512]{0:T(512)}, u32[]{:S(2)}) copy-start(f32[512]{0:T(512)} %copy-done.42) | copy-start | bytes 6148
  780.6 170.6 %copy-start.45 = (f32[512]{0:T(512)S(1)}, f32[512]{0:T(512)}, u32[]{:S(2)}) copy-start(f32[512]{0:T(512)} %copy-done.44) | copy-start | bytes 6148
  780.6 231.7 %reduce-scatter.10.cloned.1.call-start = ((), (), s32[]{:S(2)}) async-start(), calls=%async_computation.13 | async-start | bytes 3145728 | tf_op jit(solution)/shard_map/reduce_scatter | solution.py:372
  781.4 342.2 %reduce-scatter.22.cloned.1.call-start = ((), (), s32[]{:S(2)}) async-start(), calls=%async_computation.19 | async-start | bytes 540672
  954.5 309.2 %reduce-scatter.16.cloned.1.call-start = ((), (), s32[]{:S(2)}) async-start(), calls=%async_computation.16 | async-start | bytes 4325376 | tf_op jit(solution)/shard_map/reduce_scatter | solution.py:393
  955.1 468.8 %reduce-scatter.14.cloned.1.call-start = ((), (), s32[]{:S(2)}) async-start(), calls=%async_computation.15 | async-start | bytes 12976128 | tf_op jit(solution)/shard_map/reduce_scatter | solution.py:392
  967.9 814.7 %reduce-scatter.20.cloned.1.call-start = ((), (), s32[]{:S(2)}) async-start(), calls=%async_computation.18 | async-start | bytes 17301504 | tf_op jit(solution)/shard_map/reduce_scatter | solution.py:395
  968.5 1175.0 %reduce-scatter.18.cloned.1.call-start = ((), (), s32[]{:S(2)}) async-start(), calls=%async_computation.17 | async-start | bytes 17301504 | tf_op jit(solution)/shard_map/reduce_scatter | solution.py:394
  968.5 1.4 copy-start.46
  968.5 41.9 %copy-start.48 = (f32[160]{0:T(256)S(1)}, f32[160]{0:T(256)}, u32[]{:S(2)}) copy-start(f32[160]{0:T(256)} %param.59) | copy-start | bytes 1924
  968.5 41.9 %copy-start.49 = (f32[160]{0:T(256)S(1)}, f32[160]{0:T(256)}, u32[]{:S(2)}) copy-start(f32[160]{0:T(256)} %param.71) | copy-start | bytes 1924
  968.5 41.9 %copy-start.50 = (f32[160]{0:T(256)S(1)}, f32[160]{0:T(256)}, u32[]{:S(2)}) copy-start(f32[160]{0:T(256)} %param.65) | copy-start | bytes 1924
  968.6 43.8 %copy-start.21 = (bf16[512,1024]{1,0:T(8,128)(2,1)S(1)}, bf16[512,1024]{1,0:T(8,128)(2,1)}, u32[]{:S(2)}) copy-start(bf16[512,1024]{1,0:T(8,128)(2,1)} %reduce-scatter.12.cloned.1.call-done) | copy-start | bytes 3145732
  1011.8 412.2 %copy-start.32 = (f32[32,3072]{1,0:T(8,128)S(1)}, f32[32,3072]{1,0:T(8,128)}, u32[]{:S(2)}) copy-start(f32[32,3072]{1,0:T(8,128)} %param.54) | copy-start | bytes 1179652
  1012.4 770.2 %copy-start.27 = (f32[128,1024]{1,0:T(8,128)S(1)}, f32[128,1024]{1,0:T(8,128)}, u32[]{:S(2)}) copy-start(f32[128,1024]{1,0:T(8,128)} %param.57) | copy-start | bytes 1572868
  1012.4 770.2 %copy-start.35 = (f32[128,1024]{1,0:T(8,128)S(1)}, f32[128,1024]{1,0:T(8,128)}, u32[]{:S(2)}) copy-start(f32[128,1024]{1,0:T(8,128)} %param.69) | copy-start | bytes 1572868
  1016.6 766.0 %copy-start.36 = (f32[128,1024]{1,0:T(8,128)S(1)}, f32[128,1024]{1,0:T(8,128)}, u32[]{:S(2)}) copy-start(f32[128,1024]{1,0:T(8,128)} %param.63) | copy-start | bytes 1572868
  1016.6 1126.9 %copy-start.29 = (f32[32,4096]{1,0:T(8,128)S(1)}, f32[32,4096]{1,0:T(8,128)}, u32[]{:S(2)}) copy-start(f32[32,4096]{1,0:T(8,128)} %param.56) | copy-start | bytes 1572868
  1016.6 1126.9 %copy-start.37 = (f32[32,4096]{1,0:T(8,128)S(1)}, f32[32,4096]{1,0:T(8,128)}, u32[]{:S(2)}) copy-start(f32[32,4096]{1,0:T(8,128)} %param.68) | copy-start | bytes 1572868
  1016.6 1126.9 %copy-start.38 = (f32[32,4096]{1,0:T(8,128)S(1)}, f32[32,4096]{1,0:T(8,128)}, u32[]{:S(2)}) copy-start(f32[32,4096]{1,0:T(8,128)} %param.62) | copy-start | bytes 1572868
Sparse Core Ops, SparseCore 0:
  9.6 35.9 all-gather.13
  84.6 29.7 all-gather.7
  118.0 55.9 all-gather.17
  177.3 68.3 all-gather.15
  249.1 75.7 all-gather.9
  328.3 75.8 all-gather.11
  780.8 170.4 reduce-scatter.11
  954.1 32.4 reduce-scatter.9
  989.4 134.1 reduce-scatter.21
  1125.8 137.8 reduce-scatter.15
  1270.8 153.1 reduce-scatter.13
  1426.1 356.3 reduce-scatter.19
  1784.9 358.6 reduce-scatter.17
where the time goes:
time: 2160 us; the launch traced here: 2150 us
  waiting for transfers between devices  1560 us (72%)
  local copies, waits for them, and re-layouts  202 us (9%)
  blocking collectives  147 us (7%)
  matrix products  121 us (6%)
  other arithmetic  74.7 us (3%)
  loops' own time  29.2 us (1%)
    reduce_scatter x1, waiting for transfers between devices, local(): lax.psum_scatter(grad_expand, ('dp', 'branch'), scatter_dimension=0, tile...  358 us
    reduce_scatter x1, waiting for transfers between devices, local(): lax.psum_scatter(grad_shrink, ('dp', 'branch'), scatter_dimension=0, tile...  355 us
    reduce_scatter x1, waiting for transfers between devices, local(): lax.psum_scatter(dnorm_rows.astype(jnp.bfloat16), 'branch', scatter_dimen...  170 us
    reduce_scatter x1, waiting for transfers between devices, local(): lax.psum_scatter(grad_mixing, ('dp', 'branch'), scatter_dimension=0, tile...  158 us
    reduce_scatter x1, waiting for transfers between devices, local(): lax.psum_scatter(grad_merging, ('dp', 'branch'), scatter_dimension=0, til...  137 us
    unnamed x14, waiting for transfers between devices  110 us
    rev x4, local copies, waits for them, and re-layouts, swap_pairs(): return jnp.flip(shaped, axis=-1).reshape(tensor.shape)  84 us
    all_gather x1, waiting for transfers between devices, local(): lax.all_gather(shrink.astype(jnp.bfloat16), ('dp', 'branch'), axis=0, til...  79.3 us
  transfers between devices with their start and end apart: 13, of which 10 were waited for; matrix products, arithmetic and copies ran while one was open for 2% of the time, Pallas kernels for 0%

commit v1 on v0

v1 whole, which is shorter than its diff:
```python
import functools

import jax
import jax.numpy as jnp
from jax import lax
from jax.sharding import PartitionSpec as P

HEAD = 64
ROT = 32
beta_one = 0.9
beta_two = 0.95
adam_eps = 1e-08
decay_rate = 0.1
norm_eps = 1e-05
rope_base = 10000.0
masked_score = -1e30
BF = jnp.bfloat16
F32 = jnp.float32


def dot(left, right):
    return jnp.dot(left, right, preferred_element_type=F32)


def dot_left(left, right):
    return lax.dot_general(left, right, (((0,), (0,)), ((), ())), preferred_element_type=F32)


def dot_right(left, right):
    return lax.dot_general(left, right, (((1,), (1,)), ((), ())), preferred_element_type=F32)


def rope_tables(length):
    places = jnp.arange(length).astype(F32)[:, None]
    column = jnp.arange(2 * HEAD) % HEAD
    paired = (column // 2).astype(F32)
    frequency = jnp.exp(paired * (-2.0 / ROT) * jnp.log(rope_base))
    angles = places * frequency[None, :]
    inside = (column < ROT)[None, :]
    cosine = jnp.where(inside, jnp.cos(angles), 1.0)
    signed = jnp.where(column % 2 == 0, -1.0, 1.0)[None, :]
    sine = jnp.where(inside, jnp.sin(angles) * signed, 0.0)
    return cosine, sine


def adam_update(master, gradient, momentum, variance, rate, count, decay):
    drift = beta_one * momentum + (1.0 - beta_one) * gradient
    power = beta_two * variance + (1.0 - beta_two) * gradient * gradient
    first_fix = 1.0 - jnp.power(beta_one, count)
    second_fix = 1.0 - jnp.power(beta_two, count)
    moved = drift / first_fix / (jnp.sqrt(power / second_fix) + adam_eps)
    updated = master - rate * (moved + decay * master)
    return (updated, updated.astype(BF), drift, power)


class Plan:
    def __init__(self, n, stream, mixing, merging, expand, shrink, vectors, offsets):
        self.n = n
        self.own_rows, self.D = stream.shape
        self.rows = 2 * self.own_rows
        self.W = self.D // 2
        self.FF = expand.shape[1]
        self.rq = mixing.shape[0]
        self.rr = merging.shape[0]
        self.mr = max(16, self.rr)
        self.hb = shrink.shape[0]
        self.C = 4 if self.hb >= 64 else 2
        self.q = self.hb // self.C
        self.CW = self.FF // 2 // self.C
        self.wb = self.D // self.CW
        self.vc = vectors.shape[1]
        self.ow = offsets.shape[0]
        self.o_merge = 6 * self.rq
        self.o_small = self.o_merge + 2 * self.mr
        self.g_rows = self.o_small + 16
        self.c_rows = 2 * self.rq + self.wb * self.q


def pick(array, index, axis):
    return lax.dynamic_index_in_dim(array, index, axis, keepdims=False)


def small_pack(p, gain_bias, offs, plane):
    hid = pick(offs[: p.FF].reshape(p.n, 2, p.C, p.q), plane, 1)
    hid = hid.transpose(1, 0, 2).reshape(-1)
    flat = jnp.concatenate([gain_bias.reshape(-1), hid, offs[p.FF :]])
    flat = jnp.pad(flat, (0, 16 * p.W - flat.shape[0]))
    return flat.reshape(16, p.W)


def pack_for(p, plane, mixing, expand, vectors, offsets, linear):
    mix = pick(mixing.reshape(p.rq, 3, 2, p.W), plane, 2).transpose(1, 0, 2)
    exp = pick(expand.reshape(p.rq, p.n, 2, p.C, p.q), plane, 2)
    exp = exp.transpose(2, 0, 1, 3).reshape(p.C, p.rq, p.CW)
    gain_bias = lax.dynamic_update_slice(jnp.zeros((2, p.D), BF), vectors, (0, linear * p.vc))
    offs = lax.dynamic_update_slice(jnp.zeros((p.FF + p.D,), BF), offsets, (linear * p.ow,))
    return mix, exp, small_pack(p, gain_bias, offs, plane)


def swap_branch(tree):
    return jax.tree.map(lambda a: lax.ppermute(a, "branch", [(0, 1), (1, 0)]), tree)


def both(b, mine, theirs, axis):
    first = jnp.where(b == 0, mine, theirs)
    second = jnp.where(b == 0, theirs, mine)
    return jnp.concatenate([first, second], axis=axis)


def merge_perm(n):
    return [(linear, (linear % n) * 2 + linear // n) for linear in range(2 * n)]


def prepare(p, b, linear, mixing, merging, expand, shrink, vectors, offsets):
    mixing, merging, expand, shrink, vectors, offsets = (
        a.astype(BF) for a in (mixing, merging, expand, shrink, vectors, offsets)
    )
    keep = pack_for(p, b, mixing, expand, vectors, offsets, linear)
    give = pack_for(p, 1 - b, mixing, expand, vectors, offsets, linear)
    got = swap_branch(give)
    mix = both(b, keep[0], got[0], 1).reshape(6 * p.rq, p.W)
    small = keep[2] + got[2]
    mer = lax.ppermute(merging, ("dp", "branch"), merge_perm(p.n))
    mer = mer.reshape(p.rr, 2, p.W).transpose(1, 0, 2)
    mer = jnp.pad(mer, ((0, 0), (0, p.mr - p.rr), (0, 0))).reshape(2 * p.mr, p.W)
    group = jnp.concatenate([mix, mer, small], axis=0)
    exp = both(b, keep[1], got[1], 1)
    shr = shrink.reshape(p.C, p.q, p.wb, p.CW).transpose(0, 2, 1, 3).reshape(p.C, -1, p.CW)
    chunks = jnp.concatenate([exp, shr], axis=1)
    return group, chunks


def swap_pairs(tensor):
    shaped = tensor.reshape(tensor.shape[:-1] + (tensor.shape[-1] // 2, 2))
    return jnp.flip(shaped, axis=-1).reshape(tensor.shape)


def core(p, b, group, chunks, stream, cotangent, lengths):
    heads = p.W // HEAD
    full = lax.all_gather(group, "dp", axis=0)
    parts = lax.all_gather(chunks, "dp", axis=0)
    both_rows = lax.all_gather(stream, "branch", axis=0, tiled=True).astype(F32)
    grads = lax.all_gather(cotangent, "branch", axis=0, tiled=True)
    positions = jnp.arange(p.rows)
    live = positions < lengths[0]
    g = jnp.where(live[:, None], grads, jnp.zeros_like(grads))
    small = jnp.sum(full[:, p.o_small :].astype(F32), axis=0)
    flat = small.reshape(-1)
    gain, bias = flat[: p.D], flat[p.D : 2 * p.D]
    hidden_bias = flat[2 * p.D : 2 * p.D + p.FF // 2]
    tail = flat[2 * p.D + p.FF // 2 : 3 * p.D + p.FF // 2]
    wq, wk, wv = (
        full[:, t * 2 * p.rq : (t + 1) * 2 * p.rq].reshape(p.D, p.W) for t in range(3)
    )
    wo = jnp.concatenate(
        [
            full[:, p.o_merge + t * p.mr : p.o_merge + t * p.mr + p.rr].reshape(p.W, p.W)
            for t in range(2)
        ],
        axis=1,
    )
    mean = jnp.mean(both_rows, axis=1, keepdims=True)
    centred = both_rows - mean
    inverse = lax.rsqrt(jnp.mean(centred * centred, axis=1, keepdims=True) + norm_eps)
    z = centred * inverse
    normed = (z * gain + bias).astype(BF)
    cosine, sine = rope_tables(p.rows)
    cosine = jnp.tile(cosine, (1, heads // 2))
    sine = jnp.tile(sine, (1, heads // 2))

    def turn(a):
        return (a * cosine + swap_pairs(a) * sine).astype(BF)

    def turn_back(a):
        return (a * cosine + swap_pairs(a * sine)).astype(BF)

    def split(a):
        return a.reshape(p.rows, heads, HEAD)

    query = split(turn(dot(normed, wq)))
    key = split(turn(dot(normed, wk)))
    value = split(dot(normed, wv).astype(BF))
    scores = jnp.einsum("qhd,khd->hqk", query, key, preferred_element_type=F32) * HEAD**-0.5
    scores = jnp.where((positions[:, None] >= positions[None, :])[None], scores, masked_score)
    weights = jax.nn.softmax(scores, axis=2)
    rounded = weights.astype(BF)
    mixed = jnp.einsum("hqk,khd->qhd", rounded, value, preferred_element_type=F32)
    att = jnp.where(live[:, None], mixed.reshape(p.rows, p.W), 0.0).astype(BF)
    d_att = split(dot_right(g, wo).astype(BF))
    d_weights = jnp.einsum("qhd,khd->hqk", d_att, value, preferred_element_type=F32)
    delta = jnp.sum(weights * d_weights, axis=2, keepdims=True)
    d_scores = (weights * (d_weights - delta)).astype(BF)
    d_value = jnp.einsum("hqk,qhd->khd", rounded, d_att, preferred_element_type=F32)
    d_query = jnp.einsum("hqk,khd->qhd", d_scores, key, preferred_element_type=F32) * HEAD**-0.5
    d_key = jnp.einsum("hqk,qhd->khd", d_scores, query, preferred_element_type=F32) * HEAD**-0.5
    dq = turn_back(d_query.reshape(p.rows, p.W))
    dk = turn_back(d_key.reshape(p.rows, p.W))
    dv = d_value.reshape(p.rows, p.W).astype(BF)
    out = dot(att, wo)
    d_norm = dot_right(dq, wq) + dot_right(dk, wk) + dot_right(dv, wv)
    grad_mix = jnp.stack([dot_left(normed, t).reshape(p.n, 2 * p.rq, p.W) for t in (dq, dk, dv)], 1)
    grad_mer = dot_left(att, g).reshape(p.n, p.rr, 2, p.W).transpose(0, 2, 1, 3)
    grad_mer = jnp.pad(grad_mer, ((0, 0), (0, 0), (0, p.mr - p.rr), (0, 0)))
    grad_group = jnp.concatenate(
        [grad_mix.reshape(p.n, -1, p.W), grad_mer.reshape(p.n, -1, p.W)], axis=1
    )
    grad_chunks = []
    bias_grads = []
    for j in range(p.C):
        we = parts[:, j, : 2 * p.rq].reshape(p.D, p.CW)
        ws = parts[:, j, 2 * p.rq :].reshape(p.n, p.wb, p.q, p.CW).transpose(0, 2, 1, 3)
        ws = ws.reshape(p.CW, p.D)
        pre = dot(normed, we) + hidden_bias[j * p.CW : (j + 1) * p.CW]
        activated, gelu_back = jax.vjp(lambda t: jax.nn.gelu(t, approximate=True), pre)
        hidden = activated.astype(BF)
        out = out + dot(hidden, ws)
        d_pre = gelu_back(dot_right(g, ws))[0].astype(BF)
        d_norm = d_norm + dot_right(d_pre, we)
        grad_we = dot_left(normed, d_pre).reshape(p.n, 2 * p.rq, p.CW)
        grad_ws = dot_left(hidden, g).reshape(p.n, p.q, p.wb, p.CW).transpose(0, 2, 1, 3)
        grad_chunks.append(
            jnp.concatenate([grad_we, grad_ws.reshape(p.n, -1, p.CW)], axis=1)
        )
        bias_grads.append(jnp.sum(d_pre.astype(F32), axis=0))
    tail_grad = jnp.sum(g.astype(F32), axis=0)
    small_grad = jnp.concatenate(
        [jnp.sum(d_norm * z, axis=0), jnp.sum(d_norm, axis=0), *bias_grads, tail_grad]
    )
    small_grad = jnp.pad(small_grad, (0, 16 * p.W - small_grad.shape[0])).reshape(16, p.W)
    out = out + jnp.where(b == 0, tail, 0.0)
    own = lax.psum_scatter(out.astype(BF), "branch", scatter_dimension=0, tiled=True).astype(F32)
    residual = (stream.astype(F32) + own).astype(BF)
    d_own = lax.psum_scatter(d_norm.astype(BF), "branch", scatter_dimension=0, tiled=True)
    d_own = d_own.astype(F32)

    def mine(a):
        return lax.dynamic_slice_in_dim(a, b * p.own_rows, p.own_rows, 0)

    du = d_own * gain
    z_own = mine(z)
    stream_grad = mine(g).astype(F32) + mine(inverse) * (
        du
        - jnp.mean(du, axis=1, keepdims=True)
        - z_own * jnp.mean(du * z_own, axis=1, keepdims=True)
    )

    def scatter(a):
        return lax.psum_scatter(a.astype(BF), "dp", scatter_dimension=0, tiled=False).astype(F32)

    return (
        residual,
        stream_grad,
        scatter(grad_group),
        scatter(jnp.stack(grad_chunks, 1)),
        lax.psum(small_grad, "dp"),
    )


def finish(p, b, linear, group, chunks, small):
    mix = group[: 6 * p.rq].reshape(3, 2, p.rq, p.W)
    exp = chunks[:, : 2 * p.rq].reshape(p.C, 2, p.rq, p.CW)
    keep = (pick(mix, b, 1), pick(exp, b, 1), small)
    give = (pick(mix, 1 - b, 1), pick(exp, 1 - b, 1), small)
    got = swap_branch(jax.tree.map(lambda a: a.astype(BF), give[:2]) + (give[2],))

    def weave(axis, mine, theirs):
        theirs = theirs.astype(F32)
        return jnp.stack([jnp.where(b == 0, mine, theirs), jnp.where(b == 0, theirs, mine)], axis)

    grad_mixing = weave(2, keep[0].transpose(1, 0, 2), got[0].transpose(1, 0, 2))
    grad_mixing = grad_mixing.reshape(p.rq, -1)

    def columns(a):
        return a.reshape(p.C, p.rq, p.n, p.q).transpose(1, 2, 0, 3)

    grad_expand = weave(2, columns(keep[1]), columns(got[1])).reshape(p.rq, p.FF)
    mer = group[p.o_merge : p.o_merge + 2 * p.mr].reshape(2, p.mr, p.W)[:, : p.rr]
    mer = mer.transpose(1, 0, 2).reshape(p.rr, p.D)
    grad_merging = lax.ppermute(
        mer.astype(BF), ("dp", "branch"), [(t, s) for s, t in merge_perm(p.n)]
    ).astype(F32)
    shr = chunks[:, 2 * p.rq : 2 * p.rq + p.wb * p.q].reshape(p.C, p.wb, p.q, p.CW)
    grad_shrink = shr.transpose(0, 2, 1, 3).reshape(p.hb, p.D)
    mine, theirs = keep[2].reshape(-1), got[2].reshape(-1)
    total = mine + theirs
    grad_vectors = lax.dynamic_slice(
        total[: 2 * p.D].reshape(2, p.D), (0, linear * p.vc), (2, p.vc)
    )
    lo, hi = 2 * p.D, 2 * p.D + p.FF // 2

    def hidden(a):
        return a[lo:hi].reshape(p.C, p.n, p.q).transpose(1, 0, 2)

    hid = weave(1, hidden(mine), hidden(theirs)).reshape(p.FF)
    tail = mine[hi : hi + p.D]
    offs = jnp.concatenate([hid, tail])
    grad_offsets = lax.dynamic_slice(offs, (linear * p.ow,), (p.ow,))
    return grad_mixing, grad_merging, grad_expand, grad_shrink, grad_vectors, grad_offsets


def local(n, stream, cotangent, lengths, steps_taken, learning_rates, *params):
    masters, momenta, variances = params[:6], params[6:12], params[12:]
    p = Plan(n, stream, *masters)
    b = lax.axis_index("branch")
    linear = lax.axis_index("dp") * 2 + b
    group, chunks = prepare(p, b, linear, *masters)
    residual, stream_grad, group, chunks, small = core(
        p, b, group, chunks, stream, cotangent, lengths
    )
    grads = finish(p, b, linear, group, chunks, small)
    count = steps_taken[0].astype(F32)
    outs = [residual, stream_grad]
    for k in range(6):
        decay = decay_rate if k < 4 else 0.0
        outs.extend(
            adam_update(
                masters[k], grads[k], momenta[k], variances[k], learning_rates[k], count, decay
            )
        )
    return tuple(outs)


def solution(mesh):
    rows = P(("dp", "branch"), None)
    cols = P(None, ("dp", "branch"))
    flat = P(("dp", "branch"))
    six = (rows, rows, rows, rows, cols, flat)
    return jax.shard_map(
        functools.partial(local, mesh.shape["dp"]),
        mesh=mesh,
        in_specs=(rows, rows, P("dp"), P(), P()) + six * 3,
        out_specs=(rows, rows) + sum(((s,) * 4 for s in six), ()),
        check_vma=False,
    )
```

time: 2160 us -> 679 us (0.31)
  waiting for transfers between devices: 1560 us -> 150 us
  blocking collectives: 147 us -> 61.2 us
  matrix products: 121 us -> 191 us
  local copies, waits for them, and re-layouts: 202 us -> 140 us
  loops' own time: 29.2 us -> 0 us
    reduce_scatter x6 -> x4, waiting for transfers between devices: 1180 us -> 49.2 us  [the longest x2 49.2 us: scatter(): lax.psum_scatter(a.astype(BF), 'dp', scatter_dimension=0, tiled=False)]
    all_gather x6 -> x4, waiting for transfers between devices: 275 us -> 88.5 us  [the longest x1 46.6 us: core(): full = lax.all_gather(group, 'dp', axis=0)]
    unnamed x14 -> x8, waiting for transfers between devices: 110 us -> 1.48 us
    unnamed x2 -> x0, blocking collectives: 77.3 us -> none
    all_gather x1 -> x0, blocking collectives: 69.3 us -> none  [local(): lax.all_gather(vectors.astype(jnp.bfloat16), ('dp', 'branch'), axis=1, ti...]
    psum x0 -> x1, blocking collectives: none -> 61.2 us  [core(): lax.psum(small_grad, 'dp')]
    dot_general x14 -> x41, matrix products: 121 us -> 172 us  [the longest x12 43.3 us: dot_right(): lax.dot_general(left, right, (((1,), (1,)), ((), ())), preferred_element_...]
    rev x4, local copies, waits for them, and re-layouts: 84 us -> 44.2 us  [swap_pairs(): return jnp.flip(shaped, axis=-1).reshape(tensor.shape)]
  transfers between devices with their start and end apart: 13 -> 16, of which waited for: 10 -> 8; matrix products, arithmetic and copies ran while one was open for 2% -> 60% of each run, Pallas kernels for 0% -> 0%
where the time goes in v1:
time: 679 us; the launch traced here: 669 us
  matrix products  191 us (28%)
  waiting for transfers between devices  150 us (22%)
  local copies, waits for them, and re-layouts  140 us (21%)
  other arithmetic  92.7 us (14%)
  blocking collectives  61.2 us (9%)
  between operations  17.7 us (3%)
  starting transfers between devices  16.5 us (2%)
    psum x1, blocking collectives, core(): lax.psum(small_grad, 'dp')  61.2 us
    reduce_scatter x2, waiting for transfers between devices, scatter(): lax.psum_scatter(a.astype(BF), 'dp', scatter_dimension=0, tiled=False)  49.2 us
    all_gather x1, waiting for transfers between devices, core(): full = lax.all_gather(group, 'dp', axis=0)  46.6 us
    rev x4, local copies, waits for them, and re-layouts, swap_pairs(): return jnp.flip(shaped, axis=-1).reshape(tensor.shape)  44.2 us
    dot_general x12, matrix products, dot_right(): lax.dot_general(left, right, (((1,), (1,)), ((), ())), preferred_element_...  43.3 us
    all_gather x1, waiting for transfers between devices, core(): grads = lax.all_gather(cotangent, 'branch', axis=0, tiled=True)  31.8 us
    dot_general x12, matrix products, dot(): return jnp.dot(left, right, preferred_element_type=F32)  30.7 us
    convert_element_type x1, other arithmetic, core(): d_scores = (weights * (d_weights - delta)).astype(BF)  27.9 us
  transfers between devices with their start and end apart: 16, of which 8 were waited for; matrix products, arithmetic and copies ran while one was open for 60% of the time, Pallas kernels for 0%

profile of v1, /device:TPU:0, one launch (start us, length us, event | category | flops | bytes accessed | tf_op | source)
XLA Modules:
  0.0 668.5 jit_solution(10483608595740881472)
XLA Ops:
  9.4 3.0 collective-permute-start
  14.0 2.6 collective-permute-start.2
  22.1 3.2 collective-permute-start.3
  38.2 10.1 %all-gather.7.cloned.1.call-done = bf16[1024,1024]{1,0:T(8,128)(2,1)} async-done(((bf16[512,1024]{1,0:T(8,128)(2,1)}), bf16[1024,1024]{1,0:T(8,128)(2,1)}) %all-gather.7.cloned.1.call-update) | async-done | bytes 2097168 | tf_op jit(solution)/shard_map/all_gather | solution.py:142
  51.2 31.8 %all-gather.9.cloned.1.call-done = bf16[1024,1024]{1,0:T(8,128)(2,1)} async-done(((bf16[512,1024]{1,0:T(8,128)(2,1)}), bf16[1024,1024]{1,0:T(8,128)(2,1)}) %all-gather.9.cloned.1.call-update) | async-done | bytes 2097168 | tf_op jit(solution)/shard_map/all_gather | solution.py:143
  83.0 4.2 convert_reduce_fusion.1
  87.2 4.1 copy.235
  91.3 46.6 %all-gather.11.cloned.1.call-done = bf16[4352,512]{1,0:T(8,128)(2,1)} async-done(((bf16[272,512]{1,0:T(8,128)(2,1)}), bf16[4352,512]{1,0:T(8,128)(2,1)}) %all-gather.11.cloned.1.call-update) | async-done | bytes 4456464 | tf_op jit(solution)/shard_map/all_gather | solution.py:140
  138.9 3.5 fusion.100
  142.3 2.7 fusion.99
  147.8 2.6 fusion.106
  150.4 3.5 reshape.594
  153.9 11.0 %rev.13 = f32[1024,256,2]{0,2,1:T(2,128)} reverse(f32[1024,256,2]{0,2,1:T(2,128)} %reshape.594), dimensions={2} | reverse | bytes 4194304 | tf_op jit(solution)/shard_map/jit(_flip)/rev | solution.py:135
  164.9 3.7 reshape.595
  168.6 4.5 fusion.107
  173.1 3.8 reshape.598
  176.9 11.1 %rev.14 = f32[1024,256,2]{0,2,1:T(2,128)} reverse(f32[1024,256,2]{0,2,1:T(2,128)} %reshape.598), dimensions={2} | reverse | bytes 4194304 | tf_op jit(solution)/shard_map/jit(_flip)/rev | solution.py:135
  188.0 3.7 reshape.599
  191.7 4.4 convolution_convert_fusion.13
  196.1 4.5 fusion.45
  202.9 19.6 %fusion.105 = (f32[8,1024]{1,0:T(8,128)S(1)}, f32[8,1024,1024]{1,2,0:T(8,128)}) fusion(pred[1024,1024]{0,1:T(8,128)(4,1)} %iota_compare_fusion, bf16[1024,8,64]{0,2,1:T(8,128)(2,1)S(1)} %bitcast.372, bf16[1024,8,64]{0,2,1:T(8,128)(2,1)} %bitcast.374), kind=kOutput, calls=%fused_computation.243 | convolution fusion | flops 1107297280 | bytes 36732928 | tf_op jit(solution)/shard_map/sub | solution.py:185
  222.4 22.0 %multiply_reduce_fusion = (f32[8,1024]{1,0:T(8,128)S(1)}, f32[8,1024,1024]{1,2,0:T(8,128)}) fusion(f32[8,1024,1024]{1,2,0:T(8,128)} %get-tuple-element.122, f32[8,1024]{1,0:T(8,128)S(1)} %get-tuple-element.121, bf16[1024,8,64]{0,2,1:T(8,128)(2,1)} %bitcast.449, bf16[1024,8,64]{0,2,1:T(8,128)(2,1)} %bitcast.447), kind=kOutput, calls=%fused_computation.2 | convolution fusion | flops 1098899456 | bytes 69271552 | tf_op jit(solution)/shard_map/qhd,khd->hqk/dot_general | solution.py:190
  244.5 27.9 %multiply_convert_fusion = bf16[8,1024,1024]{1,2,0:T(8,128)(2,1)} fusion(f32[8,1024,1024]{1,2,0:T(8,128)} %get-tuple-element.124, f32[8,1024]{1,0:T(8,128)S(1)} %get-tuple-element.123, f32[8,1024,1024]{1,2,0:T(8,128)} %get-tuple-element.122, f32[8,1024]{1,0:T(8,128)S(1)} %get-tuple-element.121), kind=kLoop, calls=%fused_computation.1 | loop fusion | flops 33554432 | bytes 83951616 | tf_op jit(solution)/shard_map/convert_element_type | solution.py:192
  272.4 10.4 %multiply_bitcast_fusion.1 = f32[1024,8,64]{0,2,1:T(8,128)} fusion(bf16[1024,8,64]{0,2,1:T(8,128)(2,1)} %bitcast.375, bf16[8,1024,1024]{1,2,0:T(8,128)(2,1)} %multiply_convert_fusion), kind=kOutput, calls=%fused_computation.91 | convolution fusion | flops 1074266112 | bytes 19922944 | tf_op jit(solution)/shard_map/hqk,khd->qhd/dot_general | solution.py:194
  282.8 3.8 reshape.614
  286.7 12.3 %multiply_bitcast_fusion = f32[1024,8,64]{0,2,1:T(8,128)} fusion(bf16[1024,8,64]{0,2,1:T(8,128)(2,1)S(1)} %bitcast.373, bf16[8,1024,1024]{1,2,0:T(8,128)(2,1)} %multiply_convert_fusion), kind=kOutput, calls=%fused_computation.89 | convolution fusion | flops 1074266112 | bytes 19922944 | tf_op jit(solution)/shard_map/hqk,qhd->khd/dot_general | solution.py:195
  298.9 3.5 reshape.615
  302.4 6.0 fusion.101
  308.4 11.0 %rev.15 = f32[1024,256,2]{0,2,1:T(2,128)} reverse(f32[1024,256,2]{0,2,1:T(2,128)} %bitcast.346), dimensions={2} | reverse | bytes 4194304 | tf_op jit(solution)/shard_map/jit(_flip)/rev | solution.py:135
  319.4 11.1 %rev.16 = f32[1024,256,2]{0,2,1:T(2,128)} reverse(f32[1024,256,2]{0,2,1:T(2,128)} %bitcast.345), dimensions={2} | reverse | bytes 4194304 | tf_op jit(solution)/shard_map/jit(_flip)/rev | solution.py:135
  330.5 6.2 add_convert_fusion.2
  342.2 2.9 copy.207
  348.8 14.8 %fusion.48 = bf16[8,64,1024]{2,1,0:T(8,128)(2,1)} fusion(bf16[1024,8,64]{0,2,1:T(8,128)(2,1)} %bitcast.450, f32[8,1024,1024]{1,2,0:T(8,128)} %get-tuple-element.122, f32[8,1024]{1,0:T(8,128)S(1)} %get-tuple-element.121), kind=kOutput, calls=%fused_computation.98 | convolution fusion | flops 1091043328 | bytes 35684352 | tf_op jit(solution)/shard_map/hqk,qhd->khd/dot_general | solution.py:193
  363.6 2.6 fusion.53
  367.8 12.3 %fusion.7 = bf16[8,64,1024]{2,1,0:T(8,128)(2,1)S(1)} fusion(bf16[1024,8,64]{0,2,1:T(8,128)(2,1)S(1)} %bitcast.448, f32[8,1024,1024]{1,2,0:T(8,128)} %get-tuple-element.122, f32[8,1024]{1,0:T(8,128)S(1)} %get-tuple-element.121), kind=kOutput, calls=%fused_computation.13 | convolution fusion | flops 1090519040 | bytes 35684352 | tf_op jit(solution)/shard_map/hqk,khd->qhd/dot_general | solution.py:187
  386.4 4.7 fusion.113
  391.1 3.3 fusion.112
  394.4 3.3 fusion.114
  397.8 4.1 fusion.98
  414.1 2.5 convert_reduce_fusion.5
  416.6 3.7 fusion.115
  420.3 2.5 convert_reduce_fusion.4
  422.9 3.3 fusion.116
  426.2 2.5 convert_reduce_fusion.3
  428.7 3.4 fusion.117
  432.1 2.5 convert_reduce_fusion.2
  436.5 9.3 %fusion.80 = (f32[1024]{0:T(1024)S(1)}, f32[1024]{0:T(1024)S(1)}, bf16[1024,1024]{1,0:T(8,128)(2,1)}, f32[1024,1024]{1,0:T(8,128)}) fusion(f32[1024]{0:T(1024)S(1)} %copy-done.59, f32[1024]{0:T(1024)S(1)} %copy-done.56, bf16[1024,1024]{1,0:T(8,128)(2,1)S(1)} %copy-done.1, bf16[1024,512]{1,0:T(8,128)(2,1)S(1)} %get-tuple-element.41, ...), kind=kOutput, calls=%fused_computation.229 | convolution fusion | flops 1087371264 | bytes 35667968 | tf_op jit(solution)/shard_map/dot_general | solution.py:30
  446.5 4.7 fusion.56
  463.1 3.3 fusion.77
  471.5 3.4 add_convert_fusion
  475.2 4.5 convolution_convert_fusion
  483.5 2.5 convolution_convert_fusion.2
  489.5 2.6 convolution_convert_fusion.7
  499.9 4.0 pad_maximum_fusion
  508.1 3.9 collective-permute-start.4
  513.5 3.8 collective-permute-done.4
  518.2 3.0 fusion.96
  521.3 61.2 %psum.7 = f32[16,512]{1,0:T(8,128)S(1)} all-reduce(f32[16,512]{1,0:T(8,128)S(1)} %reshape.639), channel_id=1, replica_groups=mesh['dp'=16,'branch'=2] {'dp'}, use_global_device_ids=true, to_apply=%region_19.20 | all-reduce | flops 8192 | bytes 65536 | tf_op jit(solution)/shard_map/psum | solution.py:255
  582.5 3.8 collective-permute-done.7
  589.4 2.4 fusion.47
  591.9 2.7 add_convert_fusion.4
  594.6 3.6 multiply_add_fusion
  598.1 49.2 %reduce-scatter.11.cloned.1.call-done = bf16[1,4,128,512]{3,2,1,0:T(8,128)(2,1)} async-done(((bf16[16,4,128,512]{3,2,1,0:T(8,128)(2,1)}), bf16[1,4,128,512]{3,2,1,0:T(8,128)(2,1)}) %reduce-scatter.11.cloned.1.call-update) | async-done | bytes 524304 | tf_op jit(solution)/shard_map/reduce_scatter | solution.py:248
  657.9 3.3 fusion.91
  (358 shorter events, 112.9 us)
Async XLA Ops:
  7.2 5.2 copy-start.49
  7.2 5.9 copy-start.69
  7.2 6.5 copy-start.65
  7.2 41.0 %all-gather.7.cloned.1.call-start = ((), (), s32[]{:S(2)}) async-start(), calls=%async_computation.4 | async-start | bytes 3145728 | tf_op jit(solution)/shard_map/all_gather | solution.py:142
  8.0 75.0 %all-gather.9.cloned.1.call-start = ((), (), s32[]{:S(2)}) async-start(), calls=%async_computation.6 | async-start | bytes 3145728 | tf_op jit(solution)/shard_map/all_gather | solution.py:143
  8.7 129.1 %all-gather.11.cloned.1.call-start = ((), (), s32[]{:S(2)}) async-start(), calls=%async_computation.10 | async-start | bytes 4734976 | tf_op jit(solution)/shard_map/all_gather | solution.py:140
  8.8 10.6 %copy-start.21 = (f32[32,4096]{1,0:T(8,128)S(1)}, f32[32,4096]{1,0:T(8,128)}, u32[]{:S(2)}) copy-start(f32[32,4096]{1,0:T(8,128)} %param.30) | copy-start | bytes 1572868
  9.4 9.2 %collective-permute-start = (bf16[3,32,512]{2,1,0:T(8,128)(2,1)S(1)}, bf16[3,32,512]{2,1,0:T(8,128)(2,1)S(1)}, u32[]{:S(2)}, u32[]{:S(2)}) collective-permute-start(bf16[3,32,512]{2,1,0:T(8,128)(2,1)S(1)} %bitcast.427), channel_id=1, source_target_pairs={{0,1},{1,0},{2,3},{3,2},{4,5},{5,4},{6,7},{7,6},{8,9},{9,8},{10,11... | collective-permute-start | bytes 294920 | tf_op jit(solution)/shard_map/ppermute | solution.py:101
  12.4 6.1 collective-permute-start.1
  14.0 4.5 collective-permute-start.2
  19.4 378.4 %all-gather.13.cloned.1.call-start = ((), (), s32[]{:S(2)}) async-start(), calls=%async_computation.11 | async-start | bytes 8912896 | tf_op jit(solution)/shard_map/all_gather | solution.py:141
  22.1 15.1 %collective-permute-start.3 = (bf16[4,32,512]{2,1,0:T(8,128)(2,1)S(1)}, bf16[4,32,512]{2,1,0:T(8,128)(2,1)S(1)}, u32[]{:S(2)}, u32[]{:S(2)}) collective-permute-start(bf16[4,32,512]{2,1,0:T(8,128)(2,1)S(1)} %reshape.606), channel_id=1, source_target_pairs={{0,1},{1,0},{2,3},{3,2},{4,5},{5,4},{6,7},{7,6},{8,9},{9,8},{10,11... | collective-permute-start | bytes 393224 | tf_op jit(solution)/shard_map/ppermute | solution.py:101
  37.2 45.8 %copy-start.63 = (pred[1024]{0:T(1024)(128)(4,1)}, pred[1024]{0:T(1024)(128)(4,1)S(1)}, u32[]{:S(2)}) copy-start(pred[1024]{0:T(1024)(128)(4,1)S(1)} %iota_compare_fusion.1) | copy-start | bytes 3076
  38.1 467.3 %reduce-scatter.9.cloned.1.call-start = ((), (), s32[]{:S(2)}) async-start(), calls=%async_computation.8 | async-start | bytes 4456448 | tf_op jit(solution)/shard_map/reduce_scatter | solution.py:248
  50.5 289.6 %copy-start.55 = (f32[1024]{0:T(1024)}, f32[1024]{0:T(1024)S(1)}, u32[]{:S(2)}) copy-start(f32[1024]{0:T(1024)S(1)} %broadcast_multiply_fusion) | copy-start | bytes 12292
  51.2 288.9 %copy-start.58 = (f32[1024]{0:T(1024)}, f32[1024]{0:T(1024)S(1)}, u32[]{:S(2)}) copy-start(f32[1024]{0:T(1024)S(1)} %add_rsqrt_fusion) | copy-start | bytes 12292
  138.8 6.2 copy-start.57
  142.3 4.1 copy-start.44
  145.6 194.5 %copy-start.53 = (f32[1,4,2,128]{3,1,2,0:T(4,128)}, f32[1,4,2,128]{3,1,2,0:T(4,128)S(1)}, u32[]{:S(2)}) copy-start(f32[1,4,2,128]{3,1,2,0:T(4,128)S(1)} %copy.239) | copy-start | bytes 12292
  191.7 4.4 copy-start.5
  191.7 4.4 copy-start.6
  191.7 4.4 copy-start.7
  196.1 4.5 copy-start.3
  196.1 4.5 copy-start.27
  196.1 4.5 copy-start.28
  367.8 12.3 %copy-start.64 = (pred[1024]{0:T(1024)(128)(4,1)S(1)}, pred[1024]{0:T(1024)(128)(4,1)}, u32[]{:S(2)}) copy-start(pred[1024]{0:T(1024)(128)(4,1)} %copy-done.63) | copy-start | bytes 3076
  386.4 4.7 copy-start.42
  386.4 4.7 copy-start.45
  397.7 191.6 %reduce-scatter.7.cloned.1.call-start = ((), (), s32[]{:S(2)}) async-start(), calls=%async_computation.7 | async-start | bytes 3145728 | tf_op jit(solution)/shard_map/reduce_scatter | solution.py:233
  397.8 4.2 copy-start.24
  403.3 9.2 %copy-start.83 = (f32[1024,512]{1,0:T(8,128)}, f32[1024,512]{1,0:T(8,128)S(1)}, u32[]{:S(2)}) copy-start(f32[1024,512]{1,0:T(8,128)S(1)} %fusion.108) | copy-start | bytes 6291460
  404.6 7.9 %copy-start.33 = (bf16[64,8,2,512]{3,1,2,0:T(8,128)(2,1)}, bf16[64,8,2,512]{3,1,2,0:T(8,128)(2,1)S(1)}, u32[]{:S(2)}) copy-start(bf16[64,8,2,512]{3,1,2,0:T(8,128)(2,1)S(1)} %copy.241) | copy-start | bytes 3145732
  406.0 14.3 %copy-start.35 = (bf16[64,8,2,512]{3,1,2,0:T(8,128)(2,1)}, bf16[64,8,2,512]{3,1,2,0:T(8,128)(2,1)S(1)}, u32[]{:S(2)}) copy-start(bf16[64,8,2,512]{3,1,2,0:T(8,128)(2,1)S(1)} %copy.242) | copy-start | bytes 3145732
  407.3 18.9 %copy-start.37 = (bf16[64,8,2,512]{3,1,2,0:T(8,128)(2,1)}, bf16[64,8,2,512]{3,1,2,0:T(8,128)(2,1)S(1)}, u32[]{:S(2)}) copy-start(bf16[64,8,2,512]{3,1,2,0:T(8,128)(2,1)S(1)} %copy.243) | copy-start | bytes 3145732
  408.7 23.4 %copy-start.9 = (bf16[64,8,2,512]{3,1,2,0:T(8,128)(2,1)}, bf16[64,8,2,512]{3,1,2,0:T(8,128)(2,1)S(1)}, u32[]{:S(2)}) copy-start(bf16[64,8,2,512]{3,1,2,0:T(8,128)(2,1)S(1)} %copy.244) | copy-start | bytes 3145732
  409.9 10.4 %copy-start.85 = (f32[1024,512]{1,0:T(8,128)}, f32[1024,512]{1,0:T(8,128)S(1)}, u32[]{:S(2)}) copy-start(f32[1024,512]{1,0:T(8,128)S(1)} %fusion.109) | copy-start | bytes 6291460
  411.2 15.0 %copy-start.80 = (f32[1024,512]{1,0:T(8,128)}, f32[1024,512]{1,0:T(8,128)S(1)}, u32[]{:S(2)}) copy-start(f32[1024,512]{1,0:T(8,128)S(1)} %fusion.110) | copy-start | bytes 6291460
  412.4 19.6 %copy-start.18 = (f32[1024,512]{1,0:T(8,128)}, f32[1024,512]{1,0:T(8,128)S(1)}, u32[]{:S(2)}) copy-start(f32[1024,512]{1,0:T(8,128)S(1)} %fusion.111) | copy-start | bytes 6291460
  416.6 3.7 copy-start.77
  428.7 3.4 copy-start.75
  432.1 4.4 copy-start.17
  432.1 4.4 copy-start.56
  432.1 4.4 copy-start.59
  434.7 11.2 %copy-start.31 = (bf16[1024,512]{1,0:T(8,128)(2,1)}, bf16[1024,512]{1,0:T(8,128)(2,1)S(1)}, u32[]{:S(2)}) copy-start(bf16[1024,512]{1,0:T(8,128)(2,1)S(1)} %get-tuple-element.41) | copy-start | bytes 3145732
  445.9 146.0 %reduce-scatter.5.cloned.1.call-start = ((), (), s32[]{:S(2)}) async-start(), calls=%async_computation.5 | async-start | bytes 3145728 | tf_op jit(solution)/shard_map/reduce_scatter | solution.py:231
  446.5 4.7 copy-start.84
  475.0 172.3 %reduce-scatter.11.cloned.1.call-start = ((), (), s32[]{:S(2)}) async-start(), calls=%async_computation.9 | async-start | bytes 8912896 | tf_op jit(solution)/shard_map/reduce_scatter | solution.py:248
  503.9 8.2 %copy-start.50 = (f32[32,1024]{1,0:T(8,128)S(1)}, f32[32,1024]{1,0:T(8,128)}, u32[]{:S(2)}) copy-start(f32[32,1024]{1,0:T(8,128)} %param.29) | copy-start | bytes 393220
  503.9 8.2 %copy-start.51 = (f32[32,1024]{1,0:T(8,128)S(1)}, f32[32,1024]{1,0:T(8,128)}, u32[]{:S(2)}) copy-start(f32[32,1024]{1,0:T(8,128)} %param.41) | copy-start | bytes 393220
  503.9 8.2 %copy-start.52 = (f32[32,1024]{1,0:T(8,128)S(1)}, f32[32,1024]{1,0:T(8,128)}, u32[]{:S(2)}) copy-start(f32[32,1024]{1,0:T(8,128)} %param.35) | copy-start | bytes 393220
  507.3 10.9 %copy-start.30 = (f32[32,3072]{1,0:T(8,128)S(1)}, f32[32,3072]{1,0:T(8,128)}, u32[]{:S(2)}) copy-start(f32[32,3072]{1,0:T(8,128)} %param.28) | copy-start | bytes 1179652
  507.3 4.8 collective-permute-start.5
  508.1 9.2 %collective-permute-start.4 = (bf16[3,32,512]{2,1,0:T(8,128)(2,1)S(1)}, bf16[3,32,512]{2,1,0:T(8,128)(2,1)S(1)}, u32[]{:S(2)}, u32[]{:S(2)}) collective-permute-start(bf16[3,32,512]{2,1,0:T(8,128)(2,1)S(1)} %fusion.68), channel_id=1, source_target_pairs={{0,1},{1,0},{2,3},{3,2},{4,5},{5,4},{6,7},{7,6},{8,9},{9,8},{10,11... | collective-permute-start | bytes 294920 | tf_op jit(solution)/shard_map/ppermute | solution.py:101
  517.4 3.8 copy-start.62
  517.7 69.0 %copy-start.66 = (f32[2,32]{1,0:T(2,128)S(1)}, f32[2,32]{1,0:T(2,128)}, u32[]{:S(2)}) copy-start(f32[2,32]{1,0:T(2,128)} %param.32) | copy-start | bytes 772
  517.7 69.0 %copy-start.67 = (f32[2,32]{1,0:T(2,128)S(1)}, f32[2,32]{1,0:T(2,128)}, u32[]{:S(2)}) copy-start(f32[2,32]{1,0:T(2,128)} %param.44) | copy-start | bytes 772
  517.7 69.0 %copy-start.68 = (f32[2,32]{1,0:T(2,128)S(1)}, f32[2,32]{1,0:T(2,128)}, u32[]{:S(2)}) copy-start(f32[2,32]{1,0:T(2,128)} %param.38) | copy-start | bytes 772
  517.8 70.3 %copy-start.70 = (f32[160]{0:T(256)S(1)}, f32[160]{0:T(256)}, u32[]{:S(2)}) copy-start(f32[160]{0:T(256)} %param.33) | copy-start | bytes 1924
  517.8 70.3 %copy-start.71 = (f32[160]{0:T(256)S(1)}, f32[160]{0:T(256)}, u32[]{:S(2)}) copy-start(f32[160]{0:T(256)} %param.45) | copy-start | bytes 1924
  517.8 70.3 %copy-start.72 = (f32[160]{0:T(256)S(1)}, f32[160]{0:T(256)}, u32[]{:S(2)}) copy-start(f32[160]{0:T(256)} %param.39) | copy-start | bytes 1924
  517.8 71.6 %copy-start.54 = (f32[1,4,2,128]{3,1,2,0:T(4,128)S(1)}, f32[1,4,2,128]{3,1,2,0:T(4,128)}, u32[]{:S(2)}) copy-start(f32[1,4,2,128]{3,1,2,0:T(4,128)} %copy-done.53) | copy-start | bytes 12292
  521.2 70.7 %copy-start.8 = (bf16[512,1024]{1,0:T(8,128)(2,1)S(1)}, bf16[512,1024]{1,0:T(8,128)(2,1)}, u32[]{:S(2)}) copy-start(bf16[512,1024]{1,0:T(8,128)(2,1)} %param.23) | copy-start | bytes 3145732
  582.4 3.9 collective-permute-start.7
  648.6 5.3 collective-permute-start.6
  (40 other events, 86.1 us)
Sparse Core Ops, SparseCore 0:
  9.6 38.6 all-gather.6
  49.8 33.1 all-gather.8
  85.8 51.9 all-gather.10
  140.4 73.4 all-gather.12
  397.8 71.1 reduce-scatter.8
  471.2 30.7 reduce-scatter.6
  504.3 33.9 reduce-scatter.4
  542.9 104.3 reduce-scatter.10

commit v2 on v1

--- a/solution.py
+++ b/solution.py
@@ -3,6 +3,8 @@
 import jax
 import jax.numpy as jnp
 from jax import lax
+from jax.experimental import pallas as pl
+from jax.experimental.pallas import tpu as pltpu
 from jax.sharding import PartitionSpec as P
 
 HEAD = 64
@@ -130,130 +132,586 @@
     return group, chunks
 
 
-def swap_pairs(tensor):
-    shaped = tensor.reshape(tensor.shape[:-1] + (tensor.shape[-1] // 2, 2))
-    return jnp.flip(shaped, axis=-1).reshape(tensor.shape)
+MESH = pl.DeviceIdType.MESH
+BLOCK = 256
+
+
+def turned(a, cosine, sine, back):
+    lanes = a.shape[1]
+    even = lax.broadcasted_iota(jnp.int32, a.shape, 1) % 2 == 0
+    t = a * sine if back else a
+    swapped = jnp.where(even, pltpu.roll(t, lanes - 1, 1), pltpu.roll(t, 1, 1))
+    return a * cosine + (swapped if back else swapped * sine)
+
+
+def tile_lanes(a, times):
+    return jnp.concatenate([a] * times, axis=1) if times > 1 else a
+
+
+def flat2(a):
+    return a.reshape(-1, a.shape[-1])
+
+
+def gelu_parts(pre):
+    root = 0.7978845608028654
+    square = pre * pre
+    t = jnp.tanh(root * pre * (1.0 + 0.044715 * square))
+    hidden = 0.5 * pre * (1.0 + t)
+    slope = 0.5 * (1.0 + t) + 0.5 * pre * (1.0 - t * t) * root * (1.0 + 0.134145 * square)
+    return hidden, slope
+
+
+def block_kernel(
+    p,
+    a_in,
+    b_in,
+    c_in,
+    stream,
+    cotangent,
+    length,
+    cos_ref,
+    sin_ref,
+    res_out,
+    sg_out,
+    ga_out,
+    gb_out,
+    gc_out,
+    gs_out,
+    wa,
+    wb,
+    wc,
+    ws,
+    x,
+    g,
+    normed,
+    lanes,
+    dk_acc,
+    dv_acc,
+    out,
+    dnorm,
+    small,
+    trade,
+    sib_a,
+    sib_b,
+    sib_c,
+    sib_s,
+    slot_a,
+    slot_b,
+    slot_c,
+    slot_s,
+    ag_send,
+    ag_recv,
+    as_send,
+    as_recv,
+    rs_send,
+    rs_recv,
+    ss_send,
+    ss_recv,
+    x_send,
+    x_recv,
+    own_sem,
+):
+    n, C, D, W, CW, rq, q = p.n, p.C, p.D, p.W, p.CW, p.rq, p.q
+    m = n // 2
+    half = m // 2
+    blocks = p.rows // BLOCK
+    pairs = W // 128
+    groups = CW // 128
+    at_q, at_k, at_v, at_att, at_da = (t * pairs for t in range(5))
+    at_hid, at_dpre = 0, groups
+    d = lax.axis_index("dp")
+    b = lax.axis_index("branch")
+    core = lax.rem(d, 2)
+    chip = d // 2
+    ring = jnp.where(lax.rem(chip, 2) == 0, chip // 2, m - 1 - chip // 2)
+    step = 1 - 2 * core
+
+    def around(k):
+        pos = lax.rem(ring + step * k + m, m)
+        return jnp.where(pos < half, 2 * pos, 2 * (m - 1 - pos) + 1)
+
+    ahead = (2 * around(1) + core, b)
+    behind = (2 * around(-1) + core, b)
+    sibling = (d + step, b)
+    partner = (d, 1 - b)
+    ways = (ahead, behind)
+
+    barrier = pltpu.get_barrier_semaphore()
+    for other in (ahead, behind, sibling, partner):
+        pl.semaphore_signal(barrier, inc=1, device_id=other, device_id_type=MESH)
+    pl.semaphore_wait(barrier, 4)
+
+    def remote(src, dst, send, recv, to):
+        return pltpu.make_async_remote_copy(
+            src_ref=src, dst_ref=dst, send_sem=send, recv_sem=recv, device_id=to, device_id_type=MESH
+        )
+
+    own_rows = pl.ds(pl.multiple_of(b * p.own_rows, p.own_rows), p.own_rows)
+    their_rows = pl.ds(pl.multiple_of((1 - b) * p.own_rows, p.own_rows), p.own_rows)
+
+    def gather_ref(k):
+        return wa if k == 0 else wb if k == 1 else wc.at[k - 2]
+
+    def last_hop(way):
+        return half - way
+
+    def gather_copy(k, way, hop):
+        shard = gather_ref(k).at[around((1 - hop) * (1 - 2 * way)), core]
+        return remote(shard, shard, ag_send.at[k, way, hop], ag_recv.at[k, way, hop], ways[way])
+
+    def gather_arrival(k, way, hop):
+        shard = gather_ref(k).at[around(-hop * (1 - 2 * way)), core]
+        return remote(shard, shard, ag_send.at[k, way, hop], ag_recv.at[k, way, hop], ways[way])
+
+    def gather_sibling(k, whose):
+        part = gather_ref(k).at[:, whose]
+        return remote(part, part, as_send.at[k], as_recv.at[k], sibling)
+
+    def gather_start(k):
+        for way in range(2):
+            gather_copy(k, way, 1).start()
+
+    def gather_event(k, hop):
+        for way in range(2):
+            if hop <= last_hop(way):
+                gather_arrival(k, way, hop).wait_recv()
+                if hop < last_hop(way):
+                    gather_copy(k, way, hop + 1).start()
+        if hop == half:
+            gather_sibling(k, core).start()
+
+    def gather_ready(k):
+        gather_sibling(k, 1 - core).wait_recv()
+
+    def gather_done(k):
+        for way in range(2):
+            for hop in range(1, last_hop(way) + 1):
+                gather_copy(k, way, hop).wait_send()
+        gather_sibling(k, core).wait_send()
+
+    def scatter_refs(k):
+        if k == 0:
+            return wa, sib_a, slot_a, ga_out, 6 * rq
+        if k == 1:
+            return wb, sib_b, slot_b, gb_out, 2 * p.mr
+        if k < C + 2:
+            return wc.at[k - 2], sib_c.at[k - 2], slot_c.at[k - 2], gc_out.at[k - 2], p.c_rows
+        return ws, sib_s, slot_s, gs_out, 16
+
+    def scatter_sibling(k):
+        whole, sib, _, _, rows = scatter_refs(k)
+        src = whole.at[:, 1 - core, pl.ds(0, rows)]
+        return remote(src, sib, ss_send.at[k], ss_recv.at[k], sibling)
+
+    def slot_of(way, hop):
+        return (hop - 1) if way == 0 else half + hop - 1
+
+    def scatter_copy(k, way, hop):
+        whole, _, slots, _, rows = scatter_refs(k)
+        target = around((last_hop(way) + 1 - hop) * (1 - 2 * way))
+        src = whole.at[target, core, pl.ds(0, rows)]
+        return remote(
+            src, slots.at[slot_of(way, hop)], rs_send.at[k, way, hop], rs_recv.at[k, way, hop], ways[way]
+        )
+
+    def scatter_event(k, hop):
+        whole, sib, slots, result, rows = scatter_refs(k)
+        if hop == 0:
+            scatter_sibling(k).start()
+            return
+        if hop == 1:
+            scatter_sibling(k).wait_recv()
+        for way in range(2):
+            if hop <= last_hop(way):
+                target = around((last_hop(way) + 1 - hop) * (1 - 2 * way))
+                here = whole.at[target, core, pl.ds(0, rows)]
+                total = here[...].astype(F32) + sib[target].astype(F32)
+                if hop > 1:
+                    scatter_copy(k, way, hop - 1).wait_recv()
+                    total = total + slots[slot_of(way, hop - 1)].astype(F32)
+                here[...] = total.astype(BF)
+                scatter_copy(k, way, hop).start()
+        if hop == half + 1:
+            total = whole[chip, core, pl.ds(0, rows)].astype(F32) + sib[chip].astype(F32)
+            for way in range(2):
+                scatter_copy(k, way, last_hop(way)).wait_recv()
+                total = total + slots[slot_of(way, last_hop(way))].astype(F32)
+            result[...] = total
+            for way in range(2):
+                for sent in range(1, last_hop(way) + 1):
+                    scatter_copy(k, way, sent).wait_send()
+            scatter_sibling(k).wait_send()
+
+    give_x = remote(stream, x.at[own_rows], x_send.at[0], x_recv.at[0], partner)
+    give_g = remote(cotangent, g.at[own_rows], x_send.at[1], x_recv.at[1], partner)
+    keep_x = pltpu.make_async_copy(stream, x.at[own_rows], own_sem.at[0])
+    keep_g = pltpu.make_async_copy(cotangent, g.at[own_rows], own_sem.at[1])
+    wa[chip, core] = a_in[...]
+    gather_start(0)
+    give_x.start()
+    wb[chip, core] = b_in[...]
+    gather_start(1)
+    give_g.start()
+    keep_x.start()
+    keep_g.start()
+    for j in range(C):
+        wc[j, chip, core] = c_in[j]
+    for hop in range(1, half + 1):
+        gather_event(0, hop)
+        gather_event(1, hop)
+        if hop == half - 1:
+            gather_start(2)
+    for j in range(1, C):
+        gather_start(2 + j)
+
+    def weight(t):
+        return flat2(wa[:, :, t * 2 * rq : (t + 1) * 2 * rq, :])
+
+    def merge_weight(t):
+        whole = wb[:, :, t * p.mr : (t + 1) * p.mr, :]
+        if p.mr == p.rr:
+            return flat2(whole)
+        whole = whole.astype(F32).reshape(n, p.mr, W)[:, : p.rr]
+        return whole.reshape(W, W).astype(BF)
+
+    keep_x.wait()
+    keep_g.wait()
+    gather_ready(0)
+    small[:16] = jnp.sum(wa[:, :, 6 * rq :, :].reshape(n, 16, W).astype(F32), axis=0)
+    give_x.wait_recv()
+    gather_ready(1)
+    give_g.wait_recv()
+
+    def wide(row):
+        return jnp.concatenate([small[row : row + 1], small[row + 1 : row + 2]], axis=1)
+
+    def unit(rows):
+        v = x[rows].astype(F32)
+        centred = v - jnp.mean(v, axis=1, keepdims=True)
+        inverse = lax.rsqrt(jnp.mean(centred * centred, axis=1, keepdims=True) + norm_eps)
+        return centred * inverse, inverse
+
+    def rows_of(i):
+        return pl.ds(pl.multiple_of(i * BLOCK, BLOCK), BLOCK)
+
+    def project(i, carry):
+        rows = rows_of(i)
+        z, _ = unit(rows)
+        nb = (z * wide(0) + wide(2)).astype(BF)
+        normed[rows] = nb
+        cosine = tile_lanes(cos_ref[rows], pairs)
+        sine = tile_lanes(sin_ref[rows], pairs)
+        query = (turned(dot(nb, weight(0)), cosine, sine, False) * HEAD**-0.5).astype(BF)
+        key = turned(dot(nb, weight(1)), cosine, sine, False).astype(BF)
+        value = dot(nb, weight(2)).astype(BF)
+        position = lax.broadcasted_iota(jnp.int32, (BLOCK, D), 0) + i * BLOCK
+        gb = jnp.where(position < length[0], g[rows].astype(F32), 0.0).astype(BF)
+        g[rows] = gb
+        da = (dot_right(gb[:, :W], merge_weight(0)) + dot_right(gb[:, W:], merge_weight(1))).astype(BF)
+        for t in range(pairs):
+            cut = slice(t * 128, (t + 1) * 128)
+            lanes[at_q + t, rows] = query[:, cut]
+            lanes[at_k + t, rows] = key[:, cut]
+            lanes[at_v + t, rows] = value[:, cut]
+            lanes[at_da + t, rows] = da[:, cut]
+        return carry
+
+    lax.fori_loop(0, blocks, project, 0)
+
+    events = []
+    for first in range(0, C, 2):
+        for hop in range(1, half + 1):
+            events += [(2 + first, hop), (3 + first, hop)]
+    slots_total = pairs * blocks
+    per_slot = -(-len(events) // slots_total)
+
+    def attend(t, carry):
+        lane = lax.broadcasted_iota(jnp.int32, (BLOCK, 128), 1)
+        for i in range(blocks):
+            rows = slice(i * BLOCK, (i + 1) * BLOCK)
+            width = (i + 1) * BLOCK
+            qb, dab = lanes[at_q + t, rows], lanes[at_da + t, rows]
+            keys, values = lanes[at_k + t, :width], lanes[at_v + t, :width]
+            zero = jnp.zeros_like(qb)
+            mixed = []
+            dquery = []
+            dkey = jnp.zeros((width, 128), F32)
+            dvalue = jnp.zeros((width, 128), F32)
+            for h in range(2):
+                mine = (lane < HEAD) if h == 0 else (lane >= HEAD)
+                qm = jnp.where(mine, qb, zero)
+                dm = jnp.where(mine, dab, zero)
+                scores = dot_right(qm, keys)
+                down = lax.broadcasted_iota(jnp.int32, (BLOCK, BLOCK), 0)
+                over = lax.broadcasted_iota(jnp.int32, (BLOCK, BLOCK), 1)
+                edge = jnp.where(down >= over, scores[:, width - BLOCK :], masked_score)
+                scores = jnp.concatenate([scores[:, : width - BLOCK], edge], axis=1) if i else edge
+                weights = jnp.exp(scores - jnp.max(scores, axis=1, keepdims=True))
+                weights = weights * (1.0 / jnp.sum(weights, axis=1, keepdims=True))
+                rounded = weights.astype(BF)
+                dweights = dot_right(dm, values)
+                delta = jnp.sum(weights * dweights, axis=1, keepdims=True)
+                dscores = (weights * (dweights - delta)).astype(BF)
+                mixed.append(dot(rounded, values))
+                dquery.append(dot(dscores, keys))
+                dvalue = dvalue + dot_left(rounded, dm)
+                dkey = dkey + dot_left(dscores, qm)
+            first = lane < HEAD
+            position = lax.broadcasted_iota(jnp.int32, (BLOCK, 128), 0) + i * BLOCK
+            whole = jnp.where(first, mixed[0], mixed[1])
+            lanes[at_att + t, rows] = jnp.where(position < length[0], whole, 0.0).astype(BF)
+            dq = jnp.where(first, dquery[0], dquery[1]) * HEAD**-0.5
+            lanes[at_q + t, rows] = turned(dq, cos_ref[rows], sin_ref[rows], True).astype(BF)
+            if i:
+                dk_acc[: width - BLOCK] += dkey[: width - BLOCK]
+                dv_acc[: width - BLOCK] += dvalue[: width - BLOCK]
+            dk_acc[rows] = dkey[width - BLOCK :]
+            dv_acc[rows] = dvalue[width - BLOCK :]
+            for t0 in range(pairs):
+                at = (t0 * blocks + i) * per_slot
+                todo = events[at : at + per_slot]
+                if todo:
+
+                    @pl.when(t == t0)
+                    def _(todo=todo):
+                        for k, hop in todo:
+                            gather_event(k, hop)
+
+        lanes[at_k + t] = turned(dk_acc[...], cos_ref[...], sin_ref[...], True).astype(BF)
+        lanes[at_v + t] = dv_acc[...].astype(BF)
+        return carry
+
+    lax.fori_loop(0, pairs, attend, 0)
+
+    def side(at, rows, count=pairs):
+        return jnp.concatenate([lanes[at + t, rows] for t in range(count)], axis=1)
+
+    def merge(i, carry):
+        rows = rows_of(i)
+        ab = side(at_att, rows)
+        out[rows, :W] = dot(ab, merge_weight(0))
+        out[rows, W:] = dot(ab, merge_weight(1))
+        total = dot_right(side(at_q, rows), weight(0))
+        total = total + dot_right(side(at_k, rows), weight(1))
+        dnorm[rows] = total + dot_right(side(at_v, rows), weight(2))
+        return carry
+
+    lax.fori_loop(0, blocks, merge, 0)
+    gather_done(0)
+    gather_done(1)
+    every = slice(0, p.rows)
+    chips = BLOCK // (4 * rq)
+
+    def mix_grads(i, carry):
+        left = normed[:, rows_of(i)]
+        where = pl.ds(i * chips, chips)
+        for t in range(3):
+            res = dot_left(left, side(t * pairs, every)).astype(BF)
+            wa[where, :, t * 2 * rq : (t + 1) * 2 * rq, :] = res.reshape(chips, 2, 2 * rq, W)
+        return carry
+
+    lax.fori_loop(0, D // BLOCK, mix_grads, 0)
+    scatter_event(0, 0)
+    merged = BLOCK // (2 * p.rr)
+    for i in range(W // BLOCK):
+        left = side(at_att + 2 * i, every, 2)
+        for t in range(2):
+            res = dot_left(left, g[:, t * W : (t + 1) * W]).reshape(merged, 2, p.rr, W)
+            if p.mr != p.rr:
+                res = jnp.concatenate([res, jnp.zeros((merged, 2, p.mr - p.rr, W), F32)], axis=2)
+            wb[i * merged : (i + 1) * merged, :, t * p.mr : (t + 1) * p.mr, :] = res.astype(BF)
+    scatter_event(1, 0)
+
+    pending = []
+    for hop in range(1, half + 2):
+        pending += [(0, hop), (1, hop)]
+
+    def hidden_bias(j):
+        at = (2 * D + j * CW) // W
+        return jnp.concatenate([small[at + t : at + t + 1] for t in range(CW // W)], axis=1)
+
+    for j in range(C):
+        here = wc.at[j]
+        gather_ready(2 + j)
+        width = -(-len(pending) // blocks)
+        queue = [pending[t * width : (t + 1) * width] for t in range(blocks)]
+
+        def feed(i, carry, here=here, j=j, queue=queue):
+            rows = rows_of(i)
+            we = flat2(here[:, :, : 2 * rq, :])
+            gb = g[rows]
+            pre = dot(normed[rows], we) + hidden_bias(j)
+            hid, slope = gelu_parts(pre)
+            hid = hid.astype(BF)
+            for t in range(groups):
+                lanes[at_hid + t, rows] = hid[:, t * 128 : (t + 1) * 128]
+            dhid = jnp.zeros((BLOCK, CW), F32)
+            for t in range(p.wb):
+                wst = flat2(here[:, :, 2 * rq + t * q : 2 * rq + (t + 1) * q, :])
+                cols = slice(t * CW, (t + 1) * CW)
+                dhid = dhid + dot_right(gb[:, cols], wst)
+                out[rows, cols] += dot(hid, wst)
+            dp = (dhid * slope).astype(BF)
+            for t in range(groups):
+                lanes[at_dpre + t, rows] = dp[:, t * 128 : (t + 1) * 128]
+            dnorm[rows] += dot_right(dp, we)
+            for i0 in range(blocks):
+                if queue[i0]:
+
+                    @pl.when(i == i0)
+                    def _(todo=queue[i0]):
+                        for k, hop in todo:
+                            scatter_event(k, hop)
+
+            return carry + jnp.sum(dp.astype(F32), axis=0, keepdims=True)
+
+        bias_grad = lax.fori_loop(0, blocks, feed, jnp.zeros((1, CW), F32))
+        at = (2 * D + j * CW) // W
+        for t in range(CW // W):
+            small[16 + at + t : 17 + at + t] = bias_grad[:, t * W : (t + 1) * W]
+        gather_done(2 + j)
+
+        def expand_grads(i, carry, here=here):
+            res = dot_left(normed[:, rows_of(i)], side(at_dpre, every, groups)).astype(BF)
+            here[pl.ds(i * chips, chips), :, : 2 * rq, :] = res.reshape(chips, 2, 2 * rq, CW)
+            return carry
+
+        lax.fori_loop(0, D // BLOCK, expand_grads, 0)
+        per = BLOCK // (2 * q)
+
+        def shrink_grads(i, carry, here=here):
+            left = side(at_hid + 2 * i, every, 2)
+            for t in range(p.wb):
+                res = dot_left(left, g[:, t * CW : (t + 1) * CW]).astype(BF)
+                cut = slice(2 * rq + t * q, 2 * rq + (t + 1) * q)
+                here[pl.ds(i * per, per), :, cut, :] = res.reshape(per, 2, q, CW)
+            return carry
+
+        lax.fori_loop(0, CW // BLOCK, shrink_grads, 0)
+        scatter_event(2 + j, 0)
+        pending = [(2 + j, hop) for hop in range(1, half + 2)]
+
+    trade[0] = out[their_rows].astype(BF)
+    give_out = remote(trade.at[0], trade.at[1], x_send.at[2], x_recv.at[2], partner)
+    give_out.start()
+    trade[2] = dnorm[their_rows].astype(BF)
+    give_dn = remote(trade.at[2], trade.at[3], x_send.at[3], x_recv.at[3], partner)
+    give_dn.start()
+
+    def vector_grads(i, carry):
+        rows = rows_of(i)
+        z, _ = unit(rows)
+        dn = dnorm[rows]
+        gain = carry[0] + jnp.sum(dn * z, axis=0, keepdims=True)
+        shift = carry[1] + jnp.sum(dn, axis=0, keepdims=True)
+        return gain, shift, carry[2] + jnp.sum(g[rows].astype(F32), axis=0, keepdims=True)
+
+    zero_row = jnp.zeros((1, D), F32)
+    sums = lax.fori_loop(0, blocks, vector_grads, (zero_row, zero_row, zero_row))
+    last = (2 * D + p.FF // 2) // W
+    for at, row in ((0, sums[0]), (2, sums[1]), (last, sums[2])):
+        small[16 + at : 17 + at] = row[:, :W]
+        small[17 + at : 18 + at] = row[:, W:]
+    small[16 + last + 2 : 32] = jnp.zeros((14 - last, W), F32)
+    ws[...] = jnp.broadcast_to(small[16:32].astype(BF)[None, None], (m, 2, 16, W))
+    scatter_event(C + 2, 0)
+    for hop in range(1, half + 2):
+        scatter_event(C + 1, hop)
+        scatter_event(C + 2, hop)
+
+    small_rows = p.own_rows // blocks
+    give_out.wait_recv()
+    give_dn.wait_recv()
+
+    def finish_rows(i, carry):
+        local = pl.ds(pl.multiple_of(i * small_rows, small_rows), small_rows)
+        rows = pl.ds(pl.multiple_of(b * p.own_rows + i * small_rows, small_rows), small_rows)
+        z, inverse = unit(rows)
+        tail = wide(last)
+        total = out[rows] + trade[1, local].astype(F32) + tail
+        res_out[local] = (x[rows].astype(F32) + total).astype(BF)
+        du = (dnorm[rows] + trade[3, local].astype(F32)) * wide(0)
+        back = du - jnp.mean(du, axis=1, keepdims=True) - z * jnp.mean(du * z, axis=1, keepdims=True)
+        sg_out[local] = g[rows].astype(F32) + inverse * back
+        return carry
+
+    lax.fori_loop(0, blocks, finish_rows, 0)
+    for copy in (give_x, give_g, give_out, give_dn):
+        copy.wait_send()
 
 
 def core(p, b, group, chunks, stream, cotangent, lengths):
-    heads = p.W // HEAD
-    full = lax.all_gather(group, "dp", axis=0)
-    parts = lax.all_gather(chunks, "dp", axis=0)
-    both_rows = lax.all_gather(stream, "branch", axis=0, tiled=True).astype(F32)
-    grads = lax.all_gather(cotangent, "branch", axis=0, tiled=True)
-    positions = jnp.arange(p.rows)
-    live = positions < lengths[0]
-    g = jnp.where(live[:, None], grads, jnp.zeros_like(grads))
-    small = jnp.sum(full[:, p.o_small :].astype(F32), axis=0)
-    flat = small.reshape(-1)
-    gain, bias = flat[: p.D], flat[p.D : 2 * p.D]
-    hidden_bias = flat[2 * p.D : 2 * p.D + p.FF // 2]
-    tail = flat[2 * p.D + p.FF // 2 : 3 * p.D + p.FF // 2]
-    wq, wk, wv = (
-        full[:, t * 2 * p.rq : (t + 1) * 2 * p.rq].reshape(p.D, p.W) for t in range(3)
+    n, C, D, W, CW, rq = p.n, p.C, p.D, p.W, p.CW, p.rq
+    m = n // 2
+    half = m // 2
+    hops = 2 * half - 1
+    rows = p.rows
+    a_rows = 6 * rq + 16
+    b_rows = 2 * p.mr
+    a_own = jnp.concatenate([group[: 6 * rq], group[p.o_small :]], axis=0)
+    b_own = group[p.o_merge : p.o_small]
+    cosine, sine = rope_tables(rows)
+    vmem = pl.BlockSpec(memory_space=pltpu.VMEM)
+    hbm = pl.BlockSpec(memory_space=pl.ANY)
+    dma = pltpu.SemaphoreType.DMA
+    V = pltpu.VMEM
+    scratch = [
+        V((m, 2, a_rows, W), BF),
+        V((m, 2, b_rows, W), BF),
+        V((C, m, 2, p.c_rows, CW), BF),
+        V((m, 2, 16, W), BF),
+        V((rows, D), BF),
+        V((rows, D), BF),
+        V((rows, D), BF),
+        V((5 * W // 128, rows, 128), BF),
+        V((rows, 128), F32),
+        V((rows, 128), F32),
+        V((rows, D), F32),
+        V((rows, D), F32),
+        V((32, W), F32),
+        V((4, p.own_rows, D), BF),
+        V((m, 6 * rq, W), BF),
+        V((m, b_rows, W), BF),
+        V((C, m, p.c_rows, CW), BF),
+        V((m, 16, W), BF),
+        V((hops, 6 * rq, W), BF),
+        V((hops, b_rows, W), BF),
+        V((C, hops, p.c_rows, CW), BF),
+        V((hops, 16, W), BF),
+        dma((C + 2, 2, half + 1)),
+        dma((C + 2, 2, half + 1)),
+        dma((C + 2,)),
+        dma((C + 2,)),
+        dma((C + 3, 2, half + 1)),
+        dma((C + 3, 2, half + 1)),
+        dma((C + 3,)),
+        dma((C + 3,)),
+        dma((4,)),
+        dma((4,)),
+        dma((2,)),
+    ]
+    shapes = (
+        jax.ShapeDtypeStruct((p.own_rows, D), BF),
+        jax.ShapeDtypeStruct((p.own_rows, D), F32),
+        jax.ShapeDtypeStruct((6 * rq, W), F32),
+        jax.ShapeDtypeStruct((b_rows, W), F32),
+        jax.ShapeDtypeStruct((C, p.c_rows, CW), F32),
+        jax.ShapeDtypeStruct((16, W), F32),
     )
-    wo = jnp.concatenate(
-        [
-            full[:, p.o_merge + t * p.mr : p.o_merge + t * p.mr + p.rr].reshape(p.W, p.W)
-            for t in range(2)
-        ],
-        axis=1,
-    )
-    mean = jnp.mean(both_rows, axis=1, keepdims=True)
-    centred = both_rows - mean
-    inverse = lax.rsqrt(jnp.mean(centred * centred, axis=1, keepdims=True) + norm_eps)
-    z = centred * inverse
-    normed = (z * gain + bias).astype(BF)
-    cosine, sine = rope_tables(p.rows)
-    cosine = jnp.tile(cosine, (1, heads // 2))
-    sine = jnp.tile(sine, (1, heads // 2))
-
-    def turn(a):
-        return (a * cosine + swap_pairs(a) * sine).astype(BF)
-
-    def turn_back(a):
-        return (a * cosine + swap_pairs(a * sine)).astype(BF)
-
-    def split(a):
-        return a.reshape(p.rows, heads, HEAD)
-
-    query = split(turn(dot(normed, wq)))
-    key = split(turn(dot(normed, wk)))
-    value = split(dot(normed, wv).astype(BF))
-    scores = jnp.einsum("qhd,khd->hqk", query, key, preferred_element_type=F32) * HEAD**-0.5
-    scores = jnp.where((positions[:, None] >= positions[None, :])[None], scores, masked_score)
-    weights = jax.nn.softmax(scores, axis=2)
-    rounded = weights.astype(BF)
-    mixed = jnp.einsum("hqk,khd->qhd", rounded, value, preferred_element_type=F32)
-    att = jnp.where(live[:, None], mixed.reshape(p.rows, p.W), 0.0).astype(BF)
-    d_att = split(dot_right(g, wo).astype(BF))
-    d_weights = jnp.einsum("qhd,khd->hqk", d_att, value, preferred_element_type=F32)
-    delta = jnp.sum(weights * d_weights, axis=2, keepdims=True)
-    d_scores = (weights * (d_weights - delta)).astype(BF)
-    d_value = jnp.einsum("hqk,qhd->khd", rounded, d_att, preferred_element_type=F32)
-    d_query = jnp.einsum("hqk,khd->qhd", d_scores, key, preferred_element_type=F32) * HEAD**-0.5
-    d_key = jnp.einsum("hqk,qhd->khd", d_scores, query, preferred_element_type=F32) * HEAD**-0.5
-    dq = turn_back(d_query.reshape(p.rows, p.W))
-    dk = turn_back(d_key.reshape(p.rows, p.W))
-    dv = d_value.reshape(p.rows, p.W).astype(BF)
-    out = dot(att, wo)
-    d_norm = dot_right(dq, wq) + dot_right(dk, wk) + dot_right(dv, wv)
-    grad_mix = jnp.stack([dot_left(normed, t).reshape(p.n, 2 * p.rq, p.W) for t in (dq, dk, dv)], 1)
-    grad_mer = dot_left(att, g).reshape(p.n, p.rr, 2, p.W).transpose(0, 2, 1, 3)
-    grad_mer = jnp.pad(grad_mer, ((0, 0), (0, 0), (0, p.mr - p.rr), (0, 0)))
-    grad_group = jnp.concatenate(
-        [grad_mix.reshape(p.n, -1, p.W), grad_mer.reshape(p.n, -1, p.W)], axis=1
-    )
-    grad_chunks = []
-    bias_grads = []
-    for j in range(p.C):
-        we = parts[:, j, : 2 * p.rq].reshape(p.D, p.CW)
-        ws = parts[:, j, 2 * p.rq :].reshape(p.n, p.wb, p.q, p.CW).transpose(0, 2, 1, 3)
-        ws = ws.reshape(p.CW, p.D)
-        pre = dot(normed, we) + hidden_bias[j * p.CW : (j + 1) * p.CW]
-        activated, gelu_back = jax.vjp(lambda t: jax.nn.gelu(t, approximate=True), pre)
-        hidden = activated.astype(BF)
-        out = out + dot(hidden, ws)
-        d_pre = gelu_back(dot_right(g, ws))[0].astype(BF)
-        d_norm = d_norm + dot_right(d_pre, we)
-        grad_we = dot_left(normed, d_pre).reshape(p.n, 2 * p.rq, p.CW)
-        grad_ws = dot_left(hidden, g).reshape(p.n, p.q, p.wb, p.CW).transpose(0, 2, 1, 3)
-        grad_chunks.append(
-            jnp.concatenate([grad_we, grad_ws.reshape(p.n, -1, p.CW)], axis=1)
-        )
-        bias_grads.append(jnp.sum(d_pre.astype(F32), axis=0))
-    tail_grad = jnp.sum(g.astype(F32), axis=0)
-    small_grad = jnp.concatenate(
-        [jnp.sum(d_norm * z, axis=0), jnp.sum(d_norm, axis=0), *bias_grads, tail_grad]
-    )
-    small_grad = jnp.pad(small_grad, (0, 16 * p.W - small_grad.shape[0])).reshape(16, p.W)
-    out = out + jnp.where(b == 0, tail, 0.0)
-    own = lax.psum_scatter(out.astype(BF), "branch", scatter_dimension=0, tiled=True).astype(F32)
-    residual = (stream.astype(F32) + own).astype(BF)
-    d_own = lax.psum_scatter(d_norm.astype(BF), "branch", scatter_dimension=0, tiled=True)
-    d_own = d_own.astype(F32)
-
-    def mine(a):
-        return lax.dynamic_slice_in_dim(a, b * p.own_rows, p.own_rows, 0)
-
-    du = d_own * gain
-    z_own = mine(z)
-    stream_grad = mine(g).astype(F32) + mine(inverse) * (
-        du
-        - jnp.mean(du, axis=1, keepdims=True)
-        - z_own * jnp.mean(du * z_own, axis=1, keepdims=True)
-    )
-
-    def scatter(a):
-        return lax.psum_scatter(a.astype(BF), "dp", scatter_dimension=0, tiled=False).astype(F32)
-
-    return (
-        residual,
-        stream_grad,
-        scatter(grad_group),
-        scatter(jnp.stack(grad_chunks, 1)),
-        lax.psum(small_grad, "dp"),
-    )
+    flops = 2 * rows * D * (6 * p.FF // 2 + 9 * W + 3 * W) + 12 * rows * rows * W
+    residual, stream_grad, ga, gb, gc, gs = pl.pallas_call(
+        functools.partial(block_kernel, p),
+        out_shape=shapes,
+        in_specs=[vmem, vmem, vmem, hbm, hbm, pl.BlockSpec(memory_space=pltpu.SMEM), vmem, vmem],
+        out_specs=tuple(vmem for _ in shapes),
+        scratch_shapes=scratch,
+        compiler_params=pltpu.CompilerParams(
+            collective_id=0, has_side_effects=True, vmem_limit_bytes=63 * 1024 * 1024
+        ),
+        cost_estimate=pl.CostEstimate(flops=flops, bytes_accessed=8 << 20, transcendentals=0),
+    )(a_own, b_own, chunks, stream, cotangent, lengths, cosine, sine)
+    grad_group = jnp.concatenate([ga, gb], axis=0)
+    return residual, stream_grad, grad_group, gc, gs
 
 
 def finish(p, b, linear, group, chunks, small):

time: 679 us -> 327 us (0.48); the launches traced: 669 us -> 324 us
  Pallas kernels: 0 us -> 265 us
  matrix products: 191 us -> 0 us
  waiting for transfers between devices: 150 us -> 0.02 us
  local copies, waits for them, and re-layouts: 140 us -> 17.6 us
  other arithmetic: 92.7 us -> 22.9 us
  blocking collectives: 61.2 us -> 0 us
  between operations: 17.7 us -> 3.05 us
    pallas_call x0 -> x1, Pallas kernels: none -> 265 us  [core(): pl.pallas_call(functools.partial(block_kernel, p), out_shape=shapes, in_s...]
    dot_general x41 -> x0, matrix products: 172 us -> none  [the longest x12 43.3 us: dot_right(): lax.dot_general(left, right, (((1,), (1,)), ((), ())), preferred_element_...]
    all_gather x4 -> x0, waiting for transfers between devices: 88.5 us -> none  [the longest x1 46.6 us: core(): full = lax.all_gather(group, 'dp', axis=0)]
    psum x1 -> x0, blocking collectives: 61.2 us -> none  [core(): lax.psum(small_grad, 'dp')]
    reduce_scatter x4 -> x0, waiting for transfers between devices: 49.2 us -> none  [the longest x2 49.2 us: scatter(): lax.psum_scatter(a.astype(BF), 'dp', scatter_dimension=0, tiled=False)]
    rev x4 -> x0, local copies, waits for them, and re-layouts: 44.2 us -> none  [swap_pairs(): return jnp.flip(shaped, axis=-1).reshape(tensor.shape)]
    convert_element_type x7 -> x1, other arithmetic: 43.6 us -> 0.91 us  [finish(): mer.astype(BF)]
    reshape x11 -> x0, local copies, waits for them, and re-layouts: 29.4 us -> none  [the longest x2 7.41 us: swap_pairs(): return jnp.flip(shaped, axis=-1).reshape(tensor.shape)]
  transfers between devices with their start and end apart: 16 -> 8, of which waited for: 8 -> 0; matrix products, arithmetic and copies ran while one was open for 60% -> 9% of each run, Pallas kernels for 0% -> 0%
where the time goes in v2:
time: 327 us; the launch traced here: 324 us
  Pallas kernels  265 us (81%)
  other arithmetic  22.9 us (7%)
  local copies, waits for them, and re-layouts  17.6 us (5%)
  starting transfers between devices  15.1 us (5%)
    pallas_call x1, Pallas kernels, core(): pl.pallas_call(functools.partial(block_kernel, p), out_shape=shapes, in_s...  265 us
    ppermute x6, starting transfers between devices, swap_branch(): lax.ppermute(a, 'branch', [(0, 1), (1, 0)])  13.7 us
    convert_element_type x6, other arithmetic, adam_update(): return (updated, updated.astype(BF), drift, power)  13.3 us
  transfers between devices with their start and end apart: 8, of which 0 were waited for; matrix products, arithmetic and copies ran while one was open for 9% of the time, Pallas kernels for 0%

profile of v2, /device:TPU:0, one launch (start us, length us, event | category | flops | bytes accessed | tf_op | source)
XLA Modules:
  0.0 323.8 jit_solution(2261315385721374322)
XLA Ops:
  0.7 0.7 convert_element_type.101
  1.4 0.2 dynamic_update_slice.9
  1.6 0.7 convert_element_type.100
  2.3 0.1 dynamic_update_slice.8
  2.5 0.1 reshape.223
  2.6 0.1 reshape.226
  2.7 0.1 reshape.224
  2.8 3.1 collective-permute-start.1
  5.9 1.0 convert_element_type.99
  6.9 0.1 reshape.220
  7.1 0.4 constant_dynamic-slice_fusion.6
  7.5 0.1 collective-permute-start
  7.6 0.7 collective-permute-start.2
  8.4 0.8 reshape.230
  9.2 0.5 constant_dynamic-slice_fusion.2
  9.7 0.1 copy.123
  9.7 0.4 reshape.232
  10.2 3.3 %collective-permute-start.3 = (bf16[4,32,512]{2,1,0:T(8,128)(2,1)S(1)}, bf16[4,32,512]{2,1,0:T(8,128)(2,1)S(1)}, u32[]{:S(2)}, u32[]{:S(2)}) collective-permute-start(bf16[4,32,512]{2,1,0:T(8,128)(2,1)S(1)} %reshape.232), channel_id=1, source_target_pairs={{0,1},{1,0},{2,3},{3,2},{4,5},{5,4},{6,7},{7,6},{8,9},{9,8},{10,11... | collective-permute-start | bytes 393224 | tf_op jit(solution)/shard_map/ppermute | solution.py:103
  13.5 3.3 %fusion.2 = (f32[1024,128]{1,0:T(8,128)}, f32[1024,128]{1,0:T(8,128)}) fusion(f32[128]{0:T(128)S(1)} %get-tuple-element.91, f32[128]{0:T(128)S(1)} %get-tuple-element.92, f32[1024]{0:T(1024)S(1)} %iota_convert_fusion, pred[128]{0:T(512)(128)(4,1)S(1)} %broadcast_compare_fusion), kind=kLoop, calls=%fused_computation.10 | loop fusion | flops 524288 | bytes 1053824 | tf_op jit(solution)/shard_map/jit(_where)/select_n | solution.py:44
  16.8 0.6 fusion.29
  17.5 0.2 reshape.233
  17.7 0.1 copy.124
  17.8 0.4 reshape.231
  19.7 0.6 copy.126
  20.4 0.7 pad_maximum_fusion.3.a_in
  21.1 0.8 pad_maximum_fusion.1.c_in
  21.9 265.2 %shard_map.422 = (bf16[512,1024]{1,0:T(8,128)(2,1)}, f32[512,1024]{1,0:T(8,128)}, f32[192,512]{1,0:T(8,128)}, f32[64,512]{1,0:T(8,128)}, f32[4,128,512]{2,1,0:T(8,128)}, /*index=5*/f32[16,512]{1,0:T(8,128)}) custom-call(bf16[208,512]{1,0:T(8,128)(2,1)} %pad_maximum_fusion.3.a_in, bf16[64,512]{1,0:T(8,128)(2,1)} %bitcast.131, ...), custom_call_target="tpu_custom_call" | custom-call | flops 45097156608 | bytes 8388608 | tf_op jit(solution)/shard_map/pallas_call | solution.py:702
  287.1 2.1 collective-permute-start.7
  289.3 0.8 slice_bitcast_fusion
  290.0 1.6 fusion.11
  291.6 0.0 collective-permute-start.4
  291.6 0.9 convert_element_type.112
  292.5 0.7 collective-permute-start.5
  293.2 0.0 copy-start.6
  293.2 0.0 copy-start.7
  293.2 1.4 fusion.28
  294.6 5.1 %collective-permute-start.6 = (bf16[4,32,512]{2,1,0:T(8,128)(2,1)S(1)}, bf16[4,32,512]{2,1,0:T(8,128)(2,1)S(1)}, u32[]{:S(2)}, u32[]{:S(2)}) collective-permute-start(bf16[4,32,512]{2,1,0:T(8,128)(2,1)S(1)} %fusion.10), channel_id=1, source_target_pairs={{0,1},{1,0},{2,3},{3,2},{4,5},{5,4},{6,7},{7,6},{8,9},{9,8},{10,11... | collective-permute-start | bytes 393224 | tf_op jit(solution)/shard_map/ppermute | solution.py:103
  299.7 0.4 copy.102
  300.1 0.1 copy.110
  300.3 2.2 fusion.19
  302.5 0.3 reshape.238
  302.7 0.6 copy.111
  303.3 0.6 slice.71
  304.0 0.1 select_n.194
  304.1 0.1 select_n.191
  304.2 0.0 copy-start.4
  304.2 0.0 copy-start.9
  304.2 0.1 reshape.242
  304.3 2.1 fusion.17
  306.4 2.1 fusion.15
  308.5 1.5 fusion.23
  310.0 0.9 fusion.6
  311.0 0.3 copy.98
  311.3 0.3 reshape.236
  311.6 1.9 fusion.26
  313.5 0.3 reshape.243
  313.8 0.2 select_bitcast_fusion.1
  314.0 0.2 pad_maximum_fusion
  314.2 1.4 copy.101
  315.5 0.0 copy-start.2
  315.5 1.9 reshape.239
  317.5 3.6 %fusion.21 = (bf16[32,4096]{1,0:T(8,128)(2,1)}, f32[32,4096]{1,0:T(8,128)}, f32[32,4096]{1,0:T(8,128)}, f32[32,4096]{1,0:T(8,128)}) fusion(f32[32,4096]{1,0:T(8,128)S(1)} %copy-done.2, f32[]{:T(128)} %bitcast.27, f32[]{:T(128)} %bitcast.26, f32[]{:T(128)} %bitcast.31, f32[32,4096]{1,0:T(8,128)S(1)} %reshape.239, f32[32,4096]{1,0:T(8,128)} %param.42, ...), kind=kLoop, calls=%fused_computation.91 | loop fusion | flops 2097152 | bytes 3932172 | tf_op jit(solution)/shard_map/convert_element_type | solution.py:55
  321.1 1.0 copy.136
  322.0 1.3 copy.137
  (67 shorter events, 0.5 us)
Async XLA Ops:
  0.7 6.9 %copy-start.8 = (f32[32,1024]{1,0:T(8,128)S(1)}, f32[32,1024]{1,0:T(8,128)}, u32[]{:S(2)}) copy-start(f32[32,1024]{1,0:T(8,128)} %param.29) | copy-start | bytes 393220
  0.7 7.6 %copy-start.1 = (f32[32,4096]{1,0:T(8,128)S(1)}, f32[32,4096]{1,0:T(8,128)}, u32[]{:S(2)}) copy-start(f32[32,4096]{1,0:T(8,128)} %param.30) | copy-start | bytes 1572868
  2.8 16.8 %collective-permute-start.1 = (bf16[16,512]{1,0:T(8,128)(2,1)S(1)}, bf16[16,512]{1,0:T(8,128)(2,1)S(1)}, u32[]{:S(2)}, u32[]{:S(2)}) collective-permute-start(bf16[16,512]{1,0:T(8,128)(2,1)S(1)} %reshape.227), channel_id=1, source_target_pairs={{0,1},{1,0},{2,3},{3,2},{4,5},{5,4},{6,7},{7,6},{8,9},{9,8},{10,11... | collective-permute-start | bytes 49160 | tf_op jit(solution)/shard_map/ppermute | solution.py:103
  7.5 12.8 %collective-permute-start = (bf16[3,32,512]{2,1,0:T(8,128)(2,1)S(1)}, bf16[3,32,512]{2,1,0:T(8,128)(2,1)S(1)}, u32[]{:S(2)}, u32[]{:S(2)}) collective-permute-start(bf16[3,32,512]{2,1,0:T(8,128)(2,1)S(1)} %bitcast.128), channel_id=1, source_target_pairs={{0,1},{1,0},{2,3},{3,2},{4,5},{5,4},{6,7},{7,6},{8,9},{9,8},{10,11... | collective-permute-start | bytes 294920 | tf_op jit(solution)/shard_map/ppermute | solution.py:103
  7.6 12.0 %collective-permute-start.2 = (bf16[32,1024]{1,0:T(8,128)(2,1)S(1)}, bf16[32,1024]{1,0:T(8,128)(2,1)S(1)}, u32[]{:S(2)}, u32[]{:S(2)}) collective-permute-start(bf16[32,1024]{1,0:T(8,128)(2,1)S(1)} %convert_element_type.102), channel_id=1, source_target_pairs={{0,0},{1,2},{2,4},{3,6},{4,8},{5,10},{6,12},{7,14},{8,16},{9,18},{... | collective-permute-start | bytes 196616 | tf_op jit(solution)/shard_map/ppermute | solution.py:125
  9.2 7.7 %copy-start.14 = (f32[6]{0:T(128)S(1)}, f32[6]{0:T(128)}, u32[]{:S(2)}) copy-start(f32[6]{0:T(128)} %param.27) | copy-start | bytes 76
  9.2 8.3 %copy-start = (f32[128,1024]{1,0:T(8,128)S(1)}, f32[128,1024]{1,0:T(8,128)}, u32[]{:S(2)}) copy-start(f32[128,1024]{1,0:T(8,128)} %param.31) | copy-start | bytes 1572868
  10.2 10.9 %collective-permute-start.3 = (bf16[4,32,512]{2,1,0:T(8,128)(2,1)S(1)}, bf16[4,32,512]{2,1,0:T(8,128)(2,1)S(1)}, u32[]{:S(2)}, u32[]{:S(2)}) collective-permute-start(bf16[4,32,512]{2,1,0:T(8,128)(2,1)S(1)} %reshape.232), channel_id=1, source_target_pairs={{0,1},{1,0},{2,3},{3,2},{4,5},{5,4},{6,7},{7,6},{8,9},{9,8},{10,11... | collective-permute-start | bytes 393224 | tf_op jit(solution)/shard_map/ppermute | solution.py:103
  287.1 16.2 %collective-permute-start.7 = (f32[16,512]{1,0:T(8,128)}, f32[16,512]{1,0:T(8,128)S(1)}, u32[]{:S(2)}, u32[]{:S(2)}) collective-permute-start(f32[16,512]{1,0:T(8,128)} %get-tuple-element.37), channel_id=1, source_target_pairs={{0,1},{1,0},{2,3},{3,2},{4,5},{5,4},{6,7},{7,6},{8,9},{9,8},{10,11... | collective-permute-start | bytes 98312 | tf_op jit(solution)/shard_map/ppermute | solution.py:103
  291.6 18.4 %collective-permute-start.4 = (bf16[3,32,512]{2,1,0:T(8,128)(2,1)}, bf16[3,32,512]{2,1,0:T(8,128)(2,1)}, u32[]{:S(2)}, u32[]{:S(2)}) collective-permute-start(bf16[3,32,512]{2,1,0:T(8,128)(2,1)} %fusion.11), channel_id=1, source_target_pairs={{0,1},{1,0},{2,3},{3,2},{4,5},{5,4},{6,7},{7,6},{8,9},{9,8},{10,11... | collective-permute-start | bytes 294920 | tf_op jit(solution)/shard_map/ppermute | solution.py:103
  292.5 16.0 %collective-permute-start.5 = (bf16[32,1024]{1,0:T(8,128)(2,1)S(1)}, bf16[32,1024]{1,0:T(8,128)(2,1)S(1)}, u32[]{:S(2)}, u32[]{:S(2)}) collective-permute-start(bf16[32,1024]{1,0:T(8,128)(2,1)S(1)} %bitcast.130), channel_id=1, source_target_pairs={{0,0},{2,1},{4,2},{6,3},{8,4},{10,5},{12,6},{14,7},{16,8},{18,9},{... | collective-permute-start | bytes 196616 | tf_op jit(solution)/shard_map/ppermute | solution.py:737
  293.2 7.0 %copy-start.6 = (f32[128,1024]{1,0:T(8,128)S(1)}, f32[128,1024]{1,0:T(8,128)}, u32[]{:S(2)}) copy-start(f32[128,1024]{1,0:T(8,128)} %param.43) | copy-start | bytes 1572868
  293.2 7.0 %copy-start.7 = (f32[128,1024]{1,0:T(8,128)S(1)}, f32[128,1024]{1,0:T(8,128)}, u32[]{:S(2)}) copy-start(f32[128,1024]{1,0:T(8,128)} %param.37) | copy-start | bytes 1572868
  294.6 18.9 %collective-permute-start.6 = (bf16[4,32,512]{2,1,0:T(8,128)(2,1)S(1)}, bf16[4,32,512]{2,1,0:T(8,128)(2,1)S(1)}, u32[]{:S(2)}, u32[]{:S(2)}) collective-permute-start(bf16[4,32,512]{2,1,0:T(8,128)(2,1)S(1)} %fusion.10), channel_id=1, source_target_pairs={{0,1},{1,0},{2,3},{3,2},{4,5},{5,4},{6,7},{7,6},{8,9},{9,8},{10,11... | collective-permute-start | bytes 393224 | tf_op jit(solution)/shard_map/ppermute | solution.py:103
  300.3 3.1 copy-start.15
  302.4 6.1 %copy-start.12 = (f32[32,1024]{1,0:T(8,128)S(1)}, f32[32,1024]{1,0:T(8,128)}, u32[]{:S(2)}) copy-start(f32[32,1024]{1,0:T(8,128)} %param.41) | copy-start | bytes 393220
  302.4 6.1 %copy-start.13 = (f32[32,1024]{1,0:T(8,128)S(1)}, f32[32,1024]{1,0:T(8,128)}, u32[]{:S(2)}) copy-start(f32[32,1024]{1,0:T(8,128)} %param.35) | copy-start | bytes 393220
  302.4 7.5 %copy-start.11 = (f32[192,512]{1,0:T(8,128)S(1)}, f32[192,512]{1,0:T(8,128)}, u32[]{:S(2)}) copy-start(f32[192,512]{1,0:T(8,128)} %get-tuple-element.34) | copy-start | bytes 1179652
  304.2 7.4 %copy-start.4 = (f32[32,3072]{1,0:T(8,128)S(1)}, f32[32,3072]{1,0:T(8,128)}, u32[]{:S(2)}) copy-start(f32[32,3072]{1,0:T(8,128)} %param.28) | copy-start | bytes 1179652
  304.2 7.4 %copy-start.9 = (f32[32,3072]{1,0:T(8,128)S(1)}, f32[32,3072]{1,0:T(8,128)}, u32[]{:S(2)}) copy-start(f32[32,3072]{1,0:T(8,128)} %param.40) | copy-start | bytes 1179652
  304.2 7.4 %copy-start.10 = (f32[32,3072]{1,0:T(8,128)S(1)}, f32[32,3072]{1,0:T(8,128)}, u32[]{:S(2)}) copy-start(f32[32,3072]{1,0:T(8,128)} %param.34) | copy-start | bytes 1179652
  315.5 1.9 copy-start.2
  317.5 3.6 %copy-start.5 = (bf16[512,1024]{1,0:T(8,128)(2,1)S(1)}, bf16[512,1024]{1,0:T(8,128)(2,1)}, u32[]{:S(2)}) copy-start(bf16[512,1024]{1,0:T(8,128)(2,1)} %get-tuple-element.121) | copy-start | bytes 3145732
  317.5 4.6 %copy-start.3 = (f32[512,1024]{1,0:T(8,128)S(1)}, f32[512,1024]{1,0:T(8,128)}, u32[]{:S(2)}) copy-start(f32[512,1024]{1,0:T(8,128)} %get-tuple-element.122) | copy-start | bytes 6291460
